TPU v7x, 128 devices: a whole 4x4x4 slice. The times are simulated.
128 devices in a mesh: row: 8 (over z, core), col: 16 (over y, x).
Axes of the slice: x: 4, y: 4, z: 4, core: 2. Of those that a mesh axis runs over, the one named last changes fastest.
Arguments:
- covariance: float32 [4, 8, 2, 16, 512, 512], P(None, 'row', None, 'col'), may hold values from 0 to 9.5, as said below
- migration: int32 [8, 16, 16], replicated, may hold values from -1 to 15, as said below
Outputs:
- factor: float32 [4, 8, 2, 16, 512, 512], P(None, 'row', None, 'col')
- offloaded: float32 [8, 16, 16, 512, 256], P('row', 'col')
Inputs may be any that keep to these rules, and one draw needn't show every extreme that they name: covariance is symmetric and positive definite, with smallest eigenvalue 0.5 or more. An entry t >= 0 of migration[r, s, d] names half t % 2 of the local tile t // 2 of device (r, s), and that tile A[i, j] has i >= j > 1; each half-tile is named at most once; migration[r, s, s] = -1.
All inputs are finite; a program needn't handle non-finite values.
Results may differ from a plain program's by a relative error of at most 0.0003.
Values sent between devices are 32-bit elements; how exact they have to be, the bound alone decides.
A program may use at most 192 MiB of HBM per device.

v0:
```python
import jax
import jax.numpy as jnp
from jax import lax
from jax.sharding import PartitionSpec as P


def spread(block, axis, owner):
    block = jnp.where(lax.axis_index(axis) == owner, block, jnp.zeros_like(block))
    return lax.psum(block, axis)


def solve_panel(lower, panel):
    count = panel.shape[0]
    block = panel.shape[1]
    wide = panel.transpose(2, 0, 1).reshape(block, count * block)
    solved = lax.linalg.triangular_solve(lower, wide, left_side=True, lower=True)
    return solved.reshape(block, count, block).transpose(1, 2, 0)


def outer_product(left, right):
    return lax.dot_general(
        left,
        right,
        (((1,), (1,)), ((), ())),
        precision=lax.Precision.HIGHEST,
        preferred_element_type=jnp.float32,
    )


def no_product(left, right):
    return jnp.zeros((left.shape[0], right.shape[0]), jnp.float32)


def subtract(tile, left, right):
    return tile - outer_product(left, right)


def keep(tile, left, right):
    return tile


def factor_tile(tile):
    return jnp.linalg.cholesky(tile)


def empty_tile(tile):
    return jnp.zeros_like(tile)


def per_device(covariance, migration):
    rows = lax.axis_size("row")
    cols = lax.axis_size("col")
    row_index = lax.axis_index("row")
    col_index = lax.axis_index("col")
    tiles = covariance[:, 0, :, 0]
    tile_rows = tiles.shape[0]
    tile_cols = tiles.shape[1]
    block = tiles.shape[-1]
    half_cols = block // 2
    global_rows = jnp.arange(tile_rows, dtype=jnp.int32) * rows + row_index
    global_cols = jnp.arange(tile_cols, dtype=jnp.int32) * cols + col_index
    tile_list = [[tiles[l, m] for m in range(tile_cols)] for l in range(tile_rows)]

    def masked(solved, lower, step):
        place = global_rows[:, None, None]
        return jnp.where(
            place > step, solved, jnp.where(place == step, lower[None], jnp.zeros_like(solved))
        )

    def panel_step(step):
        root_row = step % rows
        root_col = step % cols
        local_row = step // rows
        local_col = step // cols
        on_column = col_index == root_col
        is_root = (row_index == root_row) & on_column
        factored = lax.cond(is_root, factor_tile, empty_tile, tile_list[local_row][local_col])
        column_tiles = jnp.stack([tile_list[l][local_col] for l in range(tile_rows)])
        lower = spread(factored, "row", root_row)

        def solve_here(stack):
            return masked(solve_panel(lower, stack), lower, step)

        def skip_here(stack):
            return jnp.zeros_like(stack)

        outgoing = lax.cond(on_column, solve_here, skip_here, column_tiles)
        received = spread(outgoing, "col", root_col)
        grouped = received.reshape(tile_cols, cols // rows, block, block)
        picked = lax.dynamic_index_in_dim(grouped, col_index // rows, axis=1, keepdims=False)
        partners = spread(picked, "row", col_index % rows)
        return (received, partners)

    def place_column(step, panel):
        for l in range(tile_rows):
            for m in range(tile_cols):
                chosen = (global_cols[m] == step) & (global_rows[l] >= step)
                tile_list[l][m] = jnp.where(chosen, panel[l], tile_list[l][m])

    first_panel, first_partners = panel_step(0)
    for l in range(tile_rows):
        for m in range(tile_cols):
            active = (global_rows[l] >= global_cols[m]) & (global_cols[m] > 0)
            tile_list[l][m] = lax.cond(
                active, subtract, keep, tile_list[l][m], first_panel[l], first_partners[m]
            )
    place_column(0, first_panel)
    second_panel, second_partners = panel_step(1)
    plan_rows = lax.dynamic_index_in_dim(migration, row_index, 0, keepdims=False)
    my_plan = lax.dynamic_index_in_dim(plan_rows, col_index, 0, keepdims=False)
    chosen_out = jnp.maximum(my_plan, 0)
    live_out = my_plan >= 0
    products = []
    for l in range(tile_rows):
        for m in range(tile_cols):
            active = (global_rows[l] >= global_cols[m]) & (global_cols[m] > 1)
            product = lax.cond(
                active, outer_product, no_product, second_panel[l], second_partners[m]
            )
            tile_list[l][m] = tile_list[l][m] - product
            products.append(product)
    stacked = jnp.stack(products)
    picked = jnp.take(stacked, chosen_out // 2, axis=0)
    halves = jnp.where(
        (chosen_out % 2 == 0)[:, None, None], picked[:, :, :half_cols], picked[:, :, half_cols:]
    )
    outgoing = jnp.where(live_out[:, None, None], halves, jnp.zeros_like(halves))
    offloaded = lax.all_to_all(outgoing, "col", split_axis=0, concat_axis=0, tiled=True)
    place_column(1, second_panel)
    result_rows = []
    for l in range(tile_rows):
        result_cols = []
        for m in range(tile_cols):
            upper = global_rows[l] < global_cols[m]
            result_cols.append(jnp.where(upper, jnp.zeros_like(tile_list[l][m]), tile_list[l][m]))
        result_rows.append(jnp.stack(result_cols))
    result = jnp.stack(result_rows)
    return (result[:, None, :, None], offloaded[None, None])


def solution(mesh):
    return jax.shard_map(
        per_device,
        mesh=mesh,
        in_specs=(P(None, "row", None, "col", None, None), P()),
        out_specs=(P(None, "row", None, "col", None, None), P("row", "col", None, None, None)),
        check_vma=False,
    )
```

profile of v0, /device:TPU:103, one launch (start us, length us, event | category | flops | bytes accessed | tf_op | source)
XLA Modules:
  0.0 1063.9 jit_solution(18278794902027828453)
XLA Ops:
  7.2 8.0 slice_bitcast_fusion.24
  20.0 4.6 pad_maximum_fusion.2
  24.6 130.0 %all-reduce.8.cloned.1.call-done = f32[512,512]{1,0:T(8,128)} async-done(((f32[512,512]{1,0:T(8,128)}), f32[512,512]{1,0:T(8,128)}) %all-reduce.8.cloned.1.call-update) | async-done | bytes 1048592 | tf_op jit(solution)/shard_map/psum | solution.py:9
  154.6 10.5 conditional.21
  167.7 181.7 %all-reduce.10.cloned.1.call-done = f32[4,512,512]{2,1,0:T(8,128)} async-done(((f32[4,512,512]{2,1,0:T(8,128)}), f32[4,512,512]{2,1,0:T(8,128)}) %all-reduce.10.cloned.1.call-update) | async-done | bytes 4194320 | tf_op jit(solution)/shard_map/psum | solution.py:9
  366.7 50.6 %all-reduce.12.cloned.1.call-done = f32[2,512,512]{2,1,0:T(8,128)} async-done(((f32[2,512,512]{2,1,0:T(8,128)}), f32[2,512,512]{2,1,0:T(8,128)}) %all-reduce.12.cloned.1.call-update) | async-done | bytes 2097168 | tf_op jit(solution)/shard_map/psum | solution.py:9
  435.6 5.4 broadcast_select_fusion.8
  441.0 4.7 conditional.26
  451.3 136.6 %all-reduce.14.cloned.1.call-done = f32[512,512]{1,0:T(8,128)} async-done(((f32[512,512]{1,0:T(8,128)}), f32[512,512]{1,0:T(8,128)}) %all-reduce.14.cloned.1.call-update) | async-done | bytes 1048592 | tf_op jit(solution)/shard_map/psum | solution.py:9
  587.9 10.4 conditional.27
  600.9 184.6 %all-reduce.16.cloned.1.call-done = f32[4,512,512]{2,1,0:T(8,128)} async-done(((f32[4,512,512]{2,1,0:T(8,128)}), f32[4,512,512]{2,1,0:T(8,128)}) %all-reduce.16.cloned.1.call-update) | async-done | bytes 4194320 | tf_op jit(solution)/shard_map/psum | solution.py:9
  800.1 53.2 %all-reduce.18.cloned.1.call-done = f32[2,512,512]{2,1,0:T(8,128)} async-done(((f32[2,512,512]{2,1,0:T(8,128)}), f32[2,512,512]{2,1,0:T(8,128)}) %all-reduce.18.cloned.1.call-update) | async-done | bytes 2097168 | tf_op jit(solution)/shard_map/psum | solution.py:9
  862.7 5.3 conditional.31
  871.3 5.5 conditional.34
  877.8 5.3 conditional.36
  884.1 5.3 conditional.37
  890.4 5.3 conditional.39
  896.8 11.2 %gather_fusion = f32[16,512,512]{2,1,0:T(8,128)} fusion(f32[8,512,512]{2,1,0:T(8,128)} %constant_dynamic-update-slice_fusion.8, s32[1024]{0:T(1024)S(1)} %pad_clamp_fusion), kind=kCustom, calls=%fused_computation | custom fusion | bytes 33554496 | tf_op jit(solution)/shard_map/jit(_take)/gather | solution.py:123
  908.0 7.1 broadcast_select_fusion
  915.1 4.6 fusion.70
  919.7 5.7 all-to-all-start
  945.1 4.5 conditional.35
  969.5 79.6 %all-to-all-done = f32[16,512,256]{2,1,0:T(8,128)} async-done(((f32[16,512,256]{2,1,0:T(8,128)}), f32[16,512,256]{2,1,0:T(8,128)}, u32[]{:S(2)}, u32[]{:S(2)}) %all-to-all-start) | async-done | bytes 8388640 | tf_op jit(solution)/shard_map/all_to_all | solution.py:128
  1049.1 7.5 copy.122
  (115 shorter events, 156.4 us)
Async XLA Ops:
  7.2 147.4 %all-reduce.8.cloned.1.call-start = ((), (), s32[]{:S(2)}) async-start(), calls=%async_computation.1 | async-start | bytes 2097152 | tf_op jit(solution)/shard_map/psum | solution.py:9
  19.9 329.5 %all-reduce.10.cloned.1.call-start = ((), (), s32[]{:S(2)}) async-start(), calls=%async_computation.2 | async-start | bytes 8388608 | tf_op jit(solution)/shard_map/psum | solution.py:9
  167.6 249.7 %all-reduce.12.cloned.1.call-start = ((), (), s32[]{:S(2)}) async-start(), calls=%async_computation.3 | async-start | bytes 4194304 | tf_op jit(solution)/shard_map/psum | solution.py:9
  352.6 235.3 %all-reduce.14.cloned.1.call-start = ((), (), s32[]{:S(2)}) async-start(), calls=%async_computation.4 | async-start | bytes 2097152 | tf_op jit(solution)/shard_map/psum | solution.py:9
  441.0 5.9 copy-start.2
  446.8 338.7 %all-reduce.16.cloned.1.call-start = ((), (), s32[]{:S(2)}) async-start(), calls=%async_computation.5 | async-start | bytes 8388608 | tf_op jit(solution)/shard_map/psum | solution.py:9
  600.9 252.5 %all-reduce.18.cloned.1.call-start = ((), (), s32[]{:S(2)}) async-start(), calls=%async_computation.6 | async-start | bytes 4194304 | tf_op jit(solution)/shard_map/psum | solution.py:9
  853.4 1.9 copy-start.16
  919.7 20.7 %copy-start.13 = (f32[512,512]{1,0:T(8,128)S(1)}, f32[512,512]{1,0:T(8,128)}, u32[]{:S(2)}) copy-start(f32[512,512]{1,0:T(8,128)} %get-tuple-element.312) | copy-start | bytes 3145732
  919.7 129.4 %all-to-all-start = ((f32[16,512,256]{2,1,0:T(8,128)}), f32[16,512,256]{2,1,0:T(8,128)}, u32[]{:S(2)}, u32[]{:S(2)}) async-start(f32[16,512,256]{2,1,0:T(8,128)} %fusion.70), calls=%async_computation | async-start | bytes 16777216 | tf_op jit(solution)/shard_map/all_to_all | solution.py:128
  925.4 15.0 %copy-start.10 = (f32[512,512]{1,0:T(8,128)S(1)}, f32[512,512]{1,0:T(8,128)}, u32[]{:S(2)}) copy-start(f32[512,512]{1,0:T(8,128)} %get-tuple-element.317) | copy-start | bytes 3145732
  940.4 3.8 copy-start.14
  944.2 1.0 copy-start.11
  945.1 4.8 copy-start.6
  945.1 4.8 copy-start.8
  949.9 4.1 copy-start
  949.9 5.3 copy-start.1
  949.9 5.5 copy-start.7
  950.0 5.8 copy-start.9
  955.8 2.7 copy-start.3
  955.8 2.7 copy-start.17
  961.0 1.2 copy-start.12
  961.0 1.5 copy-start.15
Sparse Core Ops, SparseCore 0:
  20.1 134.5 all-reduce.7
  167.8 181.6 all-reduce.9
  352.7 64.5 all-reduce.11
  446.9 140.9 all-reduce.13
  601.0 184.4 all-reduce.15
  788.8 64.5 all-reduce.17
where the time goes:
time: 1080 us; the launch traced here: 1060 us
  waiting for transfers between devices  816 us (76%)
  local copies, waits for them, and re-layouts  68.7 us (6%)
  other arithmetic  57 us (5%)
  matrix products  48 us (4%)
  between operations  44.7 us (4%)
  loops' own time  23.3 us (2%)
    psum x6, waiting for transfers between devices, spread(): return lax.psum(block, axis)  737 us
    all_to_all x1, waiting for transfers between devices, per_device(): lax.all_to_all(outgoing, 'col', split_axis=0, concat_axis=0, tiled=True)  79.6 us
    dot_general x12, matrix products, outer_product(): lax.dot_general(left, right, (((1,), (1,)), ((), ())), precision=lax.Prec...  48 us
  transfers between devices with their start and end apart: 7, of which 7 were waited for; matrix products, arithmetic and copies ran while one was open for 4% of the time, Pallas kernels for 0%

commit v1 on v0

v1 whole, which is shorter than its diff:
```python
import functools

import jax
import jax.numpy as jnp
from jax import lax
from jax.experimental import pallas as pl
from jax.experimental.pallas import tpu as pltpu
from jax.sharding import PartitionSpec as P

NB = 512
QB = 128
HALF = 256
MESH = pl.DeviceIdType.MESH
EXACT = lax.Precision.HIGHEST
F32 = jnp.float32
BF16 = jnp.bfloat16
ANY = pl.BlockSpec(memory_space=pl.ANY)
VMEM = pl.BlockSpec(memory_space=pltpu.VMEM)
SMEM = pl.BlockSpec(memory_space=pltpu.SMEM)

PARTS3 = ((0, 176, 88, "xyz"), (176, 168, 88, "yzx"), (344, 168, 88, "zxy"))
PARTS2 = ((0, 256, 128, "xy"), (256, 256, 128, "yx"))
TREE_TILE = ((0, 176, "xyz"), (176, 168, "yzx"), (344, 168, "zxy"))
TREE_PANEL = ((0, 48, "xyz"), (48, 40, "yzx"), (88, 40, "zxy"))
AHEAD = 2


def dot(a, b):
    return lax.dot_general(
        a, b, (((1,), (0,)), ((), ())), precision=EXACT, preferred_element_type=F32
    )


def dot_nt(a, b):
    return lax.dot_general(
        a, b, (((1,), (1,)), ((), ())), precision=EXACT, preferred_element_type=F32
    )


def lane_spread(v, j):
    return jnp.broadcast_to(v[:, j : j + 1], (8, 128))


def row_spread(v, i):
    return jnp.broadcast_to(v[i : i + 1, :], (8, 128))


def factor128(rows):
    n = len(rows)
    lane = lax.broadcasted_iota(jnp.int32, (8, 128), 1)
    sub = lax.broadcasted_iota(jnp.int32, (8, 128), 0)
    s_rows = list(rows)
    e_rows = [jnp.where(lane == sub + 8 * i, 1.0, 0.0).astype(F32) for i in range(n)]
    upper, inverse = [], []
    zero = jnp.zeros((8, 256), F32)
    for k in range(n):
        cols = [lane_spread(s_rows[k], 8 * k + j) for j in range(8)]
        a = [[row_spread(cols[j], i) if i >= j else None for j in range(8)] for i in range(8)]
        s = [row_spread(s_rows[k], j) for j in range(8)]
        e = [row_spread(e_rows[k], j) for j in range(8)]
        r = [None] * 8
        m = [[None] * 8 for _ in range(8)]
        for j in range(0, 8, 2):
            p, b, c = a[j][j], a[j + 1][j], a[j + 1][j + 1]
            r[j] = 1.0 / p
            r[j + 1] = p * (1.0 / (p * c - b * b))
            for i in range(j + 1, 8):
                m[i][j] = a[i][j] * r[j]
            for i in range(j + 1, 8):
                a[i][j + 1] = a[i][j + 1] - m[i][j] * b
            for i in range(j + 2, 8):
                m[i][j + 1] = a[i][j + 1] * r[j + 1]
            for i in range(j + 2, 8):
                for q in range(j + 2, i + 1):
                    a[i][q] = a[i][q] - m[i][j] * a[q][j] - m[i][j + 1] * a[q][j + 1]
        for j in range(8):
            for i in range(j + 1, 8):
                s[i] = s[i] - m[i][j] * s[j]
                e[i] = e[i] - m[i][j] * e[j]
        u = jnp.zeros((8, 128), F32)
        x = u
        for j in range(8):
            scale = lax.rsqrt(a[j][j])
            u = jnp.where(sub == j, s[j] * scale, u)
            x = jnp.where(sub == j, e[j] * scale, x)
        upper.append(jnp.where(lane >= sub + 8 * k, u, 0.0))
        inverse.append(x)
        if k + 1 == n:
            continue
        ws, we = [None] * 8, [None] * 8
        for j in range(7, -1, -1):
            ws[j] = s[j] * r[j]
            we[j] = e[j] * r[j]
            for i in range(j + 1, 8):
                ws[j] = ws[j] - m[i][j] * ws[i]
                we[j] = we[j] - m[i][j] * we[i]
        last = min(n, k + 1 + AHEAD)
        if last < n:
            w, v = u * 0.0, u * 0.0
            for j in range(8):
                w = jnp.where(sub == j, ws[j], w)
                v = jnp.where(sub == j, we[j], v)
            wide = [zero] * k + [jnp.concatenate([w, v], 1)] + [zero] * (n - 1 - k)
            change = dot(jnp.concatenate(s_rows[last:], 0), jnp.concatenate(wide, 0))
        for i in range(k + 1, last):
            c = [lane_spread(s_rows[i], 8 * k + j) for j in range(8)]
            t, v = s_rows[i], e_rows[i]
            for j in range(8):
                t = t - c[j] * ws[j]
                v = v - c[j] * we[j]
            s_rows[i], e_rows[i] = t, v
        for i in range(last, n):
            g = change[8 * (i - last) : 8 * (i - last) + 8]
            s_rows[i] = s_rows[i] - g[:, :128]
            e_rows[i] = e_rows[i] - g[:, 128:]
    return jnp.concatenate(upper, 0), jnp.concatenate(inverse, 0)


def unit(ref):
    row = lax.broadcasted_iota(jnp.int32, (NB, NB), 0)
    col = lax.broadcasted_iota(jnp.int32, (NB, NB), 1)
    ref[...] = jnp.where(row == col, 1.0, 0.0).astype(F32)


def factor_panel(p, s_ref, x_ref, u_ref):
    base = pl.multiple_of(p * 128, 128)
    here = pl.ds(base, 128)
    rows = [s_ref[pl.ds(pl.multiple_of(base + 8 * i, 8), 8), here] for i in range(16)]
    upper, inverse = factor128(rows)
    across = dot(inverse, s_ref[here, :])
    place = lax.broadcasted_iota(jnp.int32, (128, NB), 1)
    u_ref[here, :] = jnp.where(place >= base + 128, across, 0.0)
    u_ref[here, here] = upper
    xrow = dot(inverse, x_ref[here, :])
    x_ref[here, :] = xrow

    @pl.when(p < 3)
    def _():
        below = dot_nt(s_ref[:, here], inverse)
        place = lax.broadcasted_iota(jnp.int32, (NB, 128), 0)
        below = jnp.where(place >= base + 128, below, 0.0)
        s_ref[...] = s_ref[...] - dot(below, across)
        x_ref[...] = x_ref[...] - dot(below, xrow)


def exchange_kernel(
    cov_ref, g_ref, r0_ref, c0_ref, x00_out, x11_out, u00_out, u11_out,
    s_ref, x_ref, u_ref, x11_ref, u11_ref, a10_ref, a11_ref, own_ref, blk_ref, tile_ref,
    local_sem, sc_send, sc_recv, tx_send, tx_recv, ta_send, ta_recv,
    row_send, row_recv, ag_send, ag_recv, sib_send, sib_recv, c_send, c_recv, near_send, near_recv,
):
    row = lax.axis_index("row")
    col = lax.axis_index("col")
    z, core = row // 2, row % 2
    y, x = col // 4, col % 4
    pos = {"x": x, "y": y, "z": z}

    def along(axis, delta):
        q = dict(pos)
        q[axis] = (q[axis] + delta) % 4
        return (q["z"] * 2 + core, q["y"] * 4 + q["x"])

    sibling = (z * 2 + (1 - core), col)

    def remote(src, dst, target, ssem, rsem):
        return pltpu.make_async_remote_copy(
            src_ref=src, dst_ref=dst, send_sem=ssem, recv_sem=rsem, device_id=target, device_id_type=MESH
        )

    def local(src, dst):
        c = pltpu.make_async_copy(src, dst, local_sem)
        c.start()
        c.wait()

    is_root = (row == 0) & (col == 0)
    source_col = (y % 2) * 8 + row
    is_source = row < 2
    self0 = is_root
    self1 = (row == 1) & (col == 1)
    selfish = self0 | self1

    def scatter_target(m, q):
        l = 2 * m + col // 8
        return (col % 8, l * 4 + q), l

    barrier = pltpu.get_barrier_semaphore()

    def greet(target):
        pl.semaphore_signal(barrier, inc=1, device_id=target, device_id_type=MESH)

    for axis in "xyz":
        for delta in (1, 2, 3):
            greet(along(axis, delta))
    greet(sibling)
    pl.when(jnp.logical_not(self0))(lambda: greet((0, source_col)))
    pl.when(jnp.logical_not(self1))(lambda: greet((1, source_col)))

    def is_self(m, q):
        target, _ = scatter_target(m, q)
        return (target[0] == row) & (target[1] == col)

    @pl.when(is_source)
    def _():
        for m in range(2):
            for q in range(4):
                target, _ = scatter_target(m, q)
                pl.when(jnp.logical_not(is_self(m, q)))(functools.partial(greet, target))

    is_source_i = is_source.astype(jnp.int32)
    selfish_i = selfish.astype(jnp.int32)
    pl.semaphore_wait(barrier, 12 + 8 * is_source_i - 2 * selfish_i)

    def scatter_copy(m, q, dst, rsem):
        target, _ = scatter_target(m, q)
        return remote(cov_ref.at[0, m, :, pl.ds(128 * q, 128)], dst, target, sc_send.at[m * 4 + q], rsem)

    for which in range(2):

        @pl.when(row == which)
        def _(which=which):
            for m in range(2):
                for q in range(4):
                    _, l = scatter_target(m, q)
                    if which == 0:
                        copy = scatter_copy(m, q, r0_ref.at[l, q], sc_recv.at[0])
                    else:
                        copy = scatter_copy(m, q, own_ref, sc_recv.at[1])
                    pl.when(jnp.logical_not(is_self(m, q)))(copy.start)

    def offsets(root):
        return {a: (pos[a] - root[a] + 4) % 4 for a in "xyz"}

    def level(order, d):
        return jnp.where(
            d[order[2]] != 0, 2, jnp.where(d[order[1]] != 0, 1, jnp.where(d[order[0]] != 0, 0, -1))
        )

    def tree(parts, root, piece, ssem, rsem):
        d = offsets(root)
        levels = [level(order, d) for (_, _, order) in parts]

        def copy(i, t, k):
            r0, n, order = parts[i]
            return remote(piece(r0, n), piece(r0, n), along(order[t], k + 1), ssem(i, t * 3 + k), rsem(i))

        def arrive(s):
            for i in range(3):

                @pl.when(levels[i] == s)
                def _(i=i):
                    copy(i, 0, 0).wait_recv()
                    for t in range(s + 1, 3):
                        for k in range(3):
                            copy(i, t, k).start()

        def begin():
            for t in range(3):
                for i in range(3):
                    for k in range(3):
                        copy(i, t, k).start()

        def sent():
            for i in range(3):
                for t in range(3):

                    @pl.when(levels[i] < t)
                    def _(i=i, t=t):
                        for k in range(3):
                            copy(i, t, k).wait_send()

        return begin, arrive, sent

    zero_root = {"x": 0, "y": 0, "z": 0}
    tile_trees = []
    for i, (ref, at) in enumerate(((a10_ref, {"x": 0, "y": 0, "z": 0}), (a11_ref, {"x": 1, "y": 0, "z": 0}))):
        tile_trees.append(
            tree(
                TREE_TILE, at,
                lambda r0, n, ref=ref: ref.at[pl.ds(r0, n), :],
                lambda j, k, i=i: ta_send.at[i, j, k],
                lambda j, i=i: ta_recv.at[i, j],
            )
        )
    def tiles_arrive(level):
        @pl.when(core == 1)
        def _():
            for t in tile_trees:
                t[1](level)

    for i, ref in enumerate((a10_ref, a11_ref)):

        @pl.when((row == 1) & (col == i))
        def _(i=i, ref=ref):
            local(cov_ref.at[0, 0], ref)
            tile_trees[i][0]()

    @pl.when(is_root)
    def _():
        local(cov_ref.at[0, 0], s_ref)
        local(s_ref.at[:, pl.ds(0, 128)], r0_ref.at[0, 0])
        unit(x11_ref)

    @pl.when(jnp.logical_not(is_root))
    def _():
        u_ref[...] = jnp.zeros((NB, NB), F32)

    @pl.when(self1)
    def _():
        local(cov_ref.at[0, 0, :, pl.ds(128, 128)], own_ref)

    @pl.when(jnp.logical_not(self0))
    def _():
        remote(r0_ref.at[y, x], r0_ref.at[y, x], (0, source_col), sc_send.at[0], sc_recv.at[0]).wait_recv()

    def gather(parts, view, own, ssem, rsem, sib=None):
        phases = len(parts[0][3])

        def part_view(order, k, delta, r0, n, c=core):
            at = {}
            for j, a in enumerate(order):
                if j < k:
                    at[a] = slice(None)
                elif j == k:
                    at[a] = (pos[a] + delta) % 4
                else:
                    at[a] = pos[a]
            return view(at, r0, n, c)

        def number(k, i):
            return (k * len(parts) + i) * 4

        def direct(k, i, j):
            r0, n, h, order = parts[i]
            m = number(k, i)
            dst = part_view(order, k, 0, r0, n)
            src = own(r0, n) if k == 0 else dst
            return remote(src, dst, along(order[k], (1, 3)[j]), ssem.at[m + j], rsem.at[m + j])

        def passed(k, i, j, back):
            r0, n, h, order = parts[i]
            m = number(k, i) + 2 + j
            q0, qn = ((r0, h), (r0 + h, n - h))[j]
            half = part_view(order, k, back, q0, qn)
            return remote(half, half, along(order[k], (1, 3)[j]), ssem.at[m], rsem.at[m])

        def send(k):
            for i in range(len(parts)):
                for j in range(2):
                    direct(k, i, j).start()

        def forward(k):
            for i, (r0, n, h, order) in enumerate(parts):
                m = number(k, i)
                for j, back in ((0, 3), (1, 1)):
                    got = part_view(order, k, back, r0, n)
                    remote(got, got, along(order[k], 1), ssem.at[m + j], rsem.at[m + j]).wait_recv()
                    passed(k, i, j, back).start()
                    if sib:
                        sib(got, 3 + k * 9 + i * 2 + j).start()

        def finish(k):
            for i, (r0, n, h, order) in enumerate(parts):
                for j in range(2):
                    passed(k, i, j, 2).wait_recv()
                if sib:
                    sib(part_view(order, k, 2, r0, n), 3 + k * 9 + 6 + i).start()

        def sent():
            for k in range(phases):
                for i in range(len(parts)):
                    for j in range(2):
                        direct(k, i, j).wait_send()
                        passed(k, i, j, 2).wait_send()

        def pair_views(c):
            views = [part_view(order, 0, 0, r0, n, c) for (r0, n, h, order) in parts]
            for k in range(phases):
                for r0, n, h, order in parts:
                    views.append(part_view(order, k, 3, r0, n, c))
                    views.append(part_view(order, k, 1, r0, n, c))
                for r0, n, h, order in parts:
                    views.append(part_view(order, k, 2, r0, n, c))
            return views

        return send, forward, finish, sent, pair_views

    row_send_step, row_forward, row_finish, row_sent, _ = gather(
        PARTS2,
        lambda at, r0, n, c: r0_ref.at[at["y"], at["x"], pl.ds(r0, n), :],
        lambda r0, n: r0_ref.at[y, x, pl.ds(r0, n), :],
        row_send, row_recv,
    )

    row_send_step(0)

    def chol_one(p, carry):
        @pl.when(is_root)
        def _():
            factor_panel(p, s_ref, x11_ref, u_ref)
            x_ref[panel_rows(p), :] = x11_ref[panel_rows(p), :]
            begin, _, sent = panel_tree(p)

            @pl.when(p > 0)
            def _():
                sent()
                to_sibling(p).wait_send()

            begin()
            to_sibling(p).start()

        @pl.when(p == 0)
        def _():
            tiles_arrive(0)
            row_forward(0)

        @pl.when(p == 1)
        def _():
            tiles_arrive(1)
            row_finish(0)
            row_send_step(1)

        @pl.when(p == 2)
        def _():
            tiles_arrive(2)

            @pl.when(core == 1)
            def _():
                for i, ref in enumerate((a10_ref, a11_ref)):
                    remote(ref, ref, sibling, near_send.at[4 + i], near_recv.at[4 + i]).start()

            row_forward(1)

        return carry

    def panel_rows(p):
        return pl.ds(pl.multiple_of(p * 128, 128), 128)

    def panel_tree(p):
        return tree(
            TREE_PANEL, zero_root,
            lambda r0, n: x_ref.at[pl.ds(pl.multiple_of(p * 128 + r0, 8), n), :],
            lambda j, k: tx_send.at[j, k],
            lambda j: tx_recv.at[p, j],
        )

    def to_sibling(p):
        return remote(x_ref.at[panel_rows(p)], x_ref.at[panel_rows(p)], sibling, near_send.at[0], near_recv.at[p])

    lax.fori_loop(0, 4, chol_one, 0)

    def receive_panel(p, carry):
        _, arrive, sent = panel_tree(p)
        for s in range(3):
            arrive(s)
        to_sibling(p).start()
        sent()
        to_sibling(p).wait_send()
        return carry

    @pl.when((core == 0) & jnp.logical_not(is_root))
    def _():
        lax.fori_loop(0, 4, receive_panel, 0)

    @pl.when(is_root)
    def _():
        panel_tree(3)[2]()
        to_sibling(3).wait_send()

    @pl.when(core == 1)
    def _():
        for p in range(4):
            to_sibling(p).wait_recv()

    @pl.when(core == 0)
    def _():
        for i, ref in enumerate((a10_ref, a11_ref)):
            remote(ref, ref, sibling, near_send.at[4 + i], near_recv.at[4 + i]).wait_recv()

    @pl.when(jnp.logical_not(self1))
    def _():
        remote(own_ref, own_ref, (1, source_col), sc_send.at[0], sc_recv.at[1]).wait_recv()

    local(r0_ref.at[y, x], blk_ref)
    lower10 = dot_nt(a10_ref[...], x_ref[...])
    own_ref[...] = own_ref[...] - dot(lower10, dot(x_ref[...], blk_ref[...]))
    s11 = a11_ref[...] - dot_nt(lower10, lower10)

    def to_sib(ref, i):
        return remote(ref, ref, sibling, sib_send.at[i], sib_recv.at[i])

    def own_part(r0, n):
        return own_ref.at[pl.ds(r0, n), :]

    send, forward, finish, sent, pair_views = gather(
        PARTS3,
        lambda at, r0, n, c: g_ref.at[at["z"], at["y"], at["x"], c, pl.ds(r0, n), :],
        own_part, ag_send, ag_recv, to_sib,
    )
    send(0)
    local(own_ref, g_ref.at[z, y, x, core])
    for i, (r0, n, h, order) in enumerate(PARTS3):
        to_sib(g_ref.at[z, y, x, core, pl.ds(r0, n), :], i).start()
    s_ref[...] = s11
    unit(x11_ref)
    row_finish(1)

    home_z, home_core = (col % 8) // 2, col % 2
    in_line = core == home_core
    up = (z - home_z + 4) % 4

    def line_copy(m, h):
        src = r0_ref.at[2 * m + col // 8] if h == 0 else c0_ref.at[m]
        return remote(src, c0_ref.at[m], along("z", 1 if m == 0 else 3), c_send.at[m], c_recv.at[m])

    def line_hop(h):
        for m in range(2):
            place = up if m == 0 else (4 - up) % 4

            @pl.when(in_line & (place == h + 1))
            def _(m=m):
                if h >= 0:
                    line_copy(m, 1).wait_recv()
                if h < 2:
                    line_copy(m, h + 1).start()
                src = r0_ref.at[2 * m + col // 8] if h < 0 else c0_ref.at[m]
                remote(src, c0_ref.at[m], sibling, c_send.at[2 + m], c_recv.at[2 + m]).start()

    line_hop(-1)

    @pl.when(in_line & (up == 0))
    def _():
        for m in range(2):
            local(r0_ref.at[2 * m + col // 8], tile_ref)
            local(tile_ref, c0_ref.at[m])

    forward(0)
    finish(0)
    send(1)

    def chol_two(p, carry):
        factor_panel(p, s_ref, x11_ref, u11_ref)

        @pl.when(p == 1)
        def _():
            forward(1)

        @pl.when(p == 2)
        def _():
            finish(1)
            send(2)
            line_hop(0)

        return carry

    lax.fori_loop(0, 4, chol_two, 0)
    line_hop(1)
    forward(2)
    line_hop(2)
    finish(2)

    x00_out[...] = x_ref[...]
    x11_out[...] = x11_ref[...]
    u00_out[...] = u_ref[...]
    u11_out[...] = u11_ref[...]

    sent()
    row_sent()
    for i, v in enumerate(pair_views(core)):
        to_sib(v, i).wait_send()
    for i, v in enumerate(pair_views(1 - core)):
        to_sib(v, i).wait_recv()

    @pl.when(core == 1)
    def _():
        for t in tile_trees:
            t[2]()
        for i, ref in enumerate((a10_ref, a11_ref)):
            remote(ref, ref, sibling, near_send.at[4 + i], near_recv.at[4 + i]).wait_send()

    for m in range(2):
        place = up if m == 0 else (4 - up) % 4

        @pl.when(in_line)
        def _(m=m):
            pl.when(place < 3)(lambda: line_copy(m, 1).wait_send())
            remote(c0_ref.at[m], c0_ref.at[m], sibling, c_send.at[2 + m], c_recv.at[2 + m]).wait_send()

        @pl.when(jnp.logical_not(in_line))
        def _(m=m):
            remote(c0_ref.at[m], c0_ref.at[m], sibling, c_send.at[2 + m], c_recv.at[2 + m]).wait_recv()

    @pl.when(is_source)
    def _():
        for m in range(2):
            for q in range(4):
                c = scatter_copy(m, q, own_ref, sc_recv.at[1])
                pl.when(jnp.logical_not(is_self(m, q)))(c.wait_send)


def split(v):
    high = v.astype(BF16)
    return high, (v - high.astype(F32)).astype(BF16)


def dot16(a, b):
    return lax.dot_general(a, b, (((1,), (0,)), ((), ())), preferred_element_type=F32)


def dot3(a_high, a_low, b_high, b_low):
    return dot16(a_high, b_high) + dot16(a_high, b_low) + dot16(a_low, b_high)


def finish_kernel(
    plan_ref, cov_ref, g_ref, r0_ref, c0_ref, x00_ref, x11_ref, u00_ref, u11_ref,
    f_ref, o_ref,
    xh_ref, xl_ref, row_buf, col_buf, tile_buf, left_ref, right_ref, half_buf, out_buf, zero_buf,
    row_sem, col_sem, tile_sem, f_sem, half_sem, o_sem,
):
    row = lax.axis_index("row")
    col = lax.axis_index("col")

    def panel_tile(i):
        return g_ref.at[(i % 8) // 2, i // 8, :, i % 2]

    def row_copy(l, k):
        src = r0_ref.at[l] if k == 0 else panel_tile(l * 8 + row)
        return pltpu.make_async_copy(src, row_buf.at[k, l], row_sem.at[k, l])

    def col_copy(m, k):
        src = c0_ref.at[m] if k == 0 else panel_tile(m * 16 + col)
        return pltpu.make_async_copy(src, col_buf.at[k, m], col_sem.at[k, m])

    def tile_copy(n):
        return pltpu.make_async_copy(cov_ref.at[n // 2, n % 2], tile_buf.at[n], tile_sem.at[n])

    def f_copy(n):
        return pltpu.make_async_copy(tile_buf.at[n], f_ref.at[n // 2, n % 2], f_sem.at[n])

    def place(n):
        return (n // 2) * 8 + row, (n % 2) * 16 + col

    def updated(n):
        i, j = place(n)
        return (j > 1) & (i >= j)

    def entry(s):
        t = plan_ref[s]
        u = jnp.maximum(t, 0)
        return t >= 0, u // 4, (u // 2) % 2, u % 2

    def half_copy(s):
        _, _, m, h = entry(s)
        j = m * 16 + s
        src = g_ref.at[(j % 8) // 2, j // 8, pl.ds(2 * h, 2), j % 2]
        return pltpu.make_async_copy(src, half_buf.at[s % 2], half_sem.at[s % 2])

    for m in range(2):
        for k in range(2):
            col_copy(m, k).start()
    for l in range(4):
        for k in range(2):
            row_copy(l, k).start()
    for n in range(8):
        pl.when(updated(n))(tile_copy(n).start)
    pl.when(entry(0)[0])(lambda: half_copy(0).start())

    for k, ref in enumerate((x00_ref, x11_ref)):
        xh_ref[k], xl_ref[k] = split(ref[...])
    zero_buf[...] = jnp.zeros((NB, HALF), F32)

    def solved(k, blocks):
        bh, bl = split(jnp.concatenate(blocks, 1))
        return dot3(xh_ref[k], xl_ref[k], bh, bl)

    def make_col(m, carry):
        for k in range(2):
            col_copy(m, k).wait()
            h, low = split(solved(k, [col_buf[k, m, q] for q in range(4)]))
            right_ref[m, k * NB : (k + 1) * NB, :] = h
            right_ref[m, (2 + k) * NB : (3 + k) * NB, :] = low
        return carry

    lax.fori_loop(0, 2, make_col, 0)

    def make_row(l, carry):
        for k in range(2):
            row_copy(l, k).wait()
            p = solved(k, [row_buf[k, l, q] for q in range(4)]).T
            h, low = split(p)
            left_ref[l, :, k * NB : (k + 1) * NB] = h
            left_ref[l, :, (2 + k) * NB : (3 + k) * NB] = low
            i = l * 8 + row

            @pl.when(col == k)
            def _():
                tile_buf[2 * l] = p

                @pl.when(i == k)
                def _():
                    tile_buf[2 * l] = (u00_ref if k == 0 else u11_ref)[...].T

                @pl.when(i < k)
                def _():
                    tile_buf[2 * l] = jnp.zeros((NB, NB), F32)

        return carry

    lax.fori_loop(0, 4, make_row, 0)

    def trailing(n, carry):
        i, j = place(n)
        l, m = n // 2, n % 2

        @pl.when(updated(n))
        def _():
            tile_copy(n).wait()
            tile_buf[n] = tile_buf[n] - dot3(
                left_ref[l, :, : 2 * NB], left_ref[l, :, 2 * NB :],
                right_ref[m, : 2 * NB, :], right_ref[m, 2 * NB :, :],
            )

        @pl.when((j > 1) & (i < j))
        def _():
            tile_buf[n] = jnp.zeros((NB, NB), F32)

        f_copy(n).start()
        return carry

    lax.fori_loop(0, 8, trailing, 0)

    def out_copy(s):
        return pltpu.make_async_copy(out_buf.at[s % 2], o_ref.at[s], o_sem.at[s % 2])

    def moved(s, carry):
        live, l, m, h = entry(s)

        @pl.when(s >= 2)
        def _():
            out_copy(s).wait()

        @pl.when((s < 15) & entry(jnp.minimum(s + 1, 15))[0])
        def _():
            half_copy(jnp.minimum(s + 1, 15)).start()

        @pl.when(live)
        def _():
            half_copy(s).wait()
            bh, bl = split(solved(1, [half_buf[s % 2, q] for q in range(2)]))
            out_buf[s % 2] = dot3(left_ref[l, :, NB : 2 * NB], left_ref[l, :, 3 * NB :], bh, bl)
            out_copy(s).start()

        @pl.when(jnp.logical_not(live))
        def _():
            pltpu.make_async_copy(zero_buf, o_ref.at[s], o_sem.at[s % 2]).start()

        return carry

    lax.fori_loop(0, 16, moved, 0)
    for s in (14, 15):
        out_copy(s).wait()
    for n in range(8):
        f_copy(n).wait()


def per_device(covariance, migration):
    cov = covariance.reshape(4, 2, NB, NB)
    row = lax.axis_index("row")
    col = lax.axis_index("col")
    plan = lax.dynamic_slice(migration, (row, 0, col), (1, 16, 1)).reshape(16)
    dma = pltpu.SemaphoreType.DMA
    square = jax.ShapeDtypeStruct((NB, NB), F32)
    g, r0, c0, x00, x11, u00, u11 = pl.pallas_call(
        exchange_kernel,
        out_shape=[
            jax.ShapeDtypeStruct((4, 4, 4, 2, NB, QB), F32),
            jax.ShapeDtypeStruct((4, 4, NB, QB), F32),
            jax.ShapeDtypeStruct((2, 4, NB, QB), F32),
            square, square, square, square,
        ],
        in_specs=[ANY],
        out_specs=[ANY] * 3 + [VMEM] * 4,
        scratch_shapes=[pltpu.VMEM((NB, NB), F32)] * 7
        + [pltpu.VMEM((NB, QB), F32)] * 2
        + [pltpu.VMEM((4, NB, QB), F32)]
        + [
            dma, dma((8,)), dma((2,)), dma((3, 9)), dma((4, 3)), dma((2, 3, 9)), dma((2, 3)),
            dma((16,)), dma((16,)), dma((36,)), dma((36,)), dma((30,)), dma((30,)),
            dma((4,)), dma((4,)), dma((6,)), dma((6,)),
        ],
        compiler_params=pltpu.CompilerParams(
            collective_id=0, has_side_effects=True, vmem_limit_bytes=48 * 2**20
        ),
        name="exchange",
    )(cov)
    factor, offloaded = pl.pallas_call(
        finish_kernel,
        out_shape=[
            jax.ShapeDtypeStruct((4, 2, NB, NB), F32),
            jax.ShapeDtypeStruct((16, NB, HALF), F32),
        ],
        in_specs=[SMEM] + [ANY] * 4 + [VMEM] * 4,
        out_specs=[ANY, ANY],
        scratch_shapes=[
            pltpu.VMEM((2, NB, NB), BF16), pltpu.VMEM((2, NB, NB), BF16),
            pltpu.VMEM((2, 4, 4, NB, QB), F32), pltpu.VMEM((2, 2, 4, NB, QB), F32),
            pltpu.VMEM((8, NB, NB), F32),
            pltpu.VMEM((4, NB, 4 * NB), BF16), pltpu.VMEM((2, 4 * NB, NB), BF16),
            pltpu.VMEM((2, 2, NB, QB), F32), pltpu.VMEM((2, NB, HALF), F32), pltpu.VMEM((NB, HALF), F32),
            dma((2, 4)), dma((2, 2)), dma((8,)), dma((8,)), dma((2,)), dma((2,)),
        ],
        compiler_params=pltpu.CompilerParams(vmem_limit_bytes=60 * 2**20),
        name="finish",
    )(plan, cov, g, r0, c0, x00, x11, u00, u11)
    return factor[:, None, :, None], offloaded[None, None]


def solution(mesh):
    return jax.shard_map(
        per_device,
        mesh=mesh,
        in_specs=(P(None, "row", None, "col", None, None), P()),
        out_specs=(P(None, "row", None, "col", None, None), P("row", "col", None, None, None)),
        check_vma=False,
    )
```

time: 1080 us -> 310 us (0.29)
  the two profiles are of different devices: /device:TPU:103 before, /device:TPU:41 now
where the time goes in v1:
time: 310 us
  Pallas kernels  303 us (98%)
  local copies, waits for them, and re-layouts  5.56 us (2%)
    pallas_call x1, Pallas kernels, per_device(): pl.pallas_call(exchange_kernel, out_shape=[jax.ShapeDtypeStruct((4, 4, 4,...  254 us
    pallas_call x1, Pallas kernels, per_device(): pl.pallas_call(finish_kernel, out_shape=[jax.ShapeDtypeStruct((4, 2, NB,...  49.3 us

profile of v1, /device:TPU:41, one launch (start us, length us, event | category | flops | bytes accessed | tf_op | source)
XLA Modules:
  0.0 309.8 jit_solution(4402144375101882909)
XLA Ops:
  0.6 0.0 copy-start
  0.7 0.8 copy-done
  1.5 0.8 dynamic-slice_reduce_fusion.plan_ref
  2.2 254.1 %exchange.1 = (f32[4,4,4,2,512,128]{5,4,3,2,1,0:T(8,128)}, f32[4,4,512,128]{3,2,1,0:T(8,128)}, f32[2,4,512,128]{3,2,1,0:T(8,128)}, f32[512,512]{1,0:T(8,128)S(1)...) custom-call(f32[4,2,512,512]{3,2,1,0:T(8,128)} %bitcast.5), custom_call_target="tpu_custom_call" | custom-call | tf_op jit(solution)/shard_map/exchange/pallas_call | solution.py:772
  256.3 0.0 copy-start.2
  256.3 1.0 copy-done.2
  257.3 0.0 copy-start.3
  257.3 1.0 copy-done.3
  258.3 0.0 copy-start.4
  258.3 1.0 copy-done.4
  259.3 0.0 copy-start.5
  259.3 1.0 copy-done.5
  260.3 0.0 copy-start.1
  260.3 49.3 %finish.1 = (f32[4,2,512,512]{3,2,1,0:T(8,128)}, f32[16,512,256]{2,1,0:T(8,128)}) custom-call(s32[16]{0:T(128)} %dynamic-slice_reduce_fusion.plan_ref, f32[4,2,512,512]{3,2,1,0:T(8,128)} %bitcast.6, f32[4,4,4,2,512,128]{5,4,3,2,1,0:T(8,128)} %get-tuple-element.11.g_ref, f32[4,4,512,128]{3,2,1,0:T(8,128)} %get-tuple-element.12.r0_ref, ...), custom_call_target="tpu_custom_call" | custom-call | tf_op jit(solution)/shard_map/finish/pallas_call | solution.py:795
  309.6 0.0 copy-done.1
Async XLA Ops:
  0.6 0.8 copy-start
  256.3 1.0 copy-start.2
  257.3 1.0 copy-start.3
  258.3 1.0 copy-start.4
  259.3 1.0 copy-start.5
  260.3 49.3 %copy-start.1 = (s32[8,16,16]{2,1,0:T(8,128)S(1)}, s32[8,16,16]{2,1,0:T(8,128)}, u32[]{:S(2)}) copy-start(s32[8,16,16]{2,1,0:T(8,128)} %param.3) | copy-start | bytes 24580

commit v2 on v1

v2 whole, which is shorter than its diff:
```python
import functools

import jax
import jax.numpy as jnp
from jax import lax
from jax.experimental import pallas as pl
from jax.experimental.pallas import tpu as pltpu
from jax.sharding import PartitionSpec as P

NB = 512
QB = 128
HALF = 256
MESH = pl.DeviceIdType.MESH
EXACT = lax.Precision.HIGHEST
F32 = jnp.float32
BF16 = jnp.bfloat16
ANY = pl.BlockSpec(memory_space=pl.ANY)
VMEM = pl.BlockSpec(memory_space=pltpu.VMEM)
SMEM = pl.BlockSpec(memory_space=pltpu.SMEM)

PARTS3 = ((0, 176, 88, "xyz"), (176, 168, 88, "yzx"), (344, 168, 88, "zxy"))
PARTS2 = ((0, 256, 128, "xy"), (256, 256, 128, "yx"))
TREE_BLOCK = ((0, 256, "xy"), (256, 256, "yx"))
TREE_PANEL = ((0, 48, "xyz"), (48, 40, "yzx"), (88, 40, "zxy"))
AHEAD = 2
SCHEDULE = sorted(((p, s) for p in range(4) for s in range(3)), key=lambda v: 5.5 * v[0] + 6.0 * v[1])


def dot(a, b):
    return lax.dot_general(
        a, b, (((1,), (0,)), ((), ())), precision=EXACT, preferred_element_type=F32
    )


def dot_nt(a, b):
    return lax.dot_general(
        a, b, (((1,), (1,)), ((), ())), precision=EXACT, preferred_element_type=F32
    )


def lane_spread(v, j):
    return jnp.broadcast_to(v[:, j : j + 1], (8, 128))


def row_spread(v, i):
    return jnp.broadcast_to(v[i : i + 1, :], (8, 128))


def factor128(rows):
    n = len(rows)
    lane = lax.broadcasted_iota(jnp.int32, (8, 128), 1)
    sub = lax.broadcasted_iota(jnp.int32, (8, 128), 0)
    s_rows = list(rows)
    e_rows = [jnp.where(lane == sub + 8 * i, 1.0, 0.0).astype(F32) for i in range(n)]
    upper, inverse = [], []
    zero = jnp.zeros((8, 256), F32)
    for k in range(n):
        cols = [lane_spread(s_rows[k], 8 * k + j) for j in range(8)]
        a = [[row_spread(cols[j], i) if i >= j else None for j in range(8)] for i in range(8)]
        s = [row_spread(s_rows[k], j) for j in range(8)]
        e = [row_spread(e_rows[k], j) for j in range(8)]
        r = [None] * 8
        m = [[None] * 8 for _ in range(8)]
        for j in range(0, 8, 2):
            p, b, c = a[j][j], a[j + 1][j], a[j + 1][j + 1]
            r[j] = 1.0 / p
            r[j + 1] = p * (1.0 / (p * c - b * b))
            for i in range(j + 1, 8):
                m[i][j] = a[i][j] * r[j]
            for i in range(j + 1, 8):
                a[i][j + 1] = a[i][j + 1] - m[i][j] * b
            for i in range(j + 2, 8):
                m[i][j + 1] = a[i][j + 1] * r[j + 1]
            for i in range(j + 2, 8):
                for q in range(j + 2, i + 1):
                    a[i][q] = a[i][q] - m[i][j] * a[q][j] - m[i][j + 1] * a[q][j + 1]
        for j in range(8):
            for i in range(j + 1, 8):
                s[i] = s[i] - m[i][j] * s[j]
                e[i] = e[i] - m[i][j] * e[j]
        u = jnp.zeros((8, 128), F32)
        x = u
        for j in range(8):
            scale = lax.rsqrt(a[j][j])
            u = jnp.where(sub == j, s[j] * scale, u)
            x = jnp.where(sub == j, e[j] * scale, x)
        upper.append(jnp.where(lane >= sub + 8 * k, u, 0.0))
        inverse.append(x)
        if k + 1 == n:
            continue
        ws, we = [None] * 8, [None] * 8
        for j in range(7, -1, -1):
            ws[j] = s[j] * r[j]
            we[j] = e[j] * r[j]
            for i in range(j + 1, 8):
                ws[j] = ws[j] - m[i][j] * ws[i]
                we[j] = we[j] - m[i][j] * we[i]
        last = min(n, k + 1 + AHEAD)
        if last < n:
            w, v = u * 0.0, u * 0.0
            for j in range(8):
                w = jnp.where(sub == j, ws[j], w)
                v = jnp.where(sub == j, we[j], v)
            wide = [zero] * k + [jnp.concatenate([w, v], 1)] + [zero] * (n - 1 - k)
            change = dot(jnp.concatenate(s_rows[last:], 0), jnp.concatenate(wide, 0))
        for i in range(k + 1, last):
            c = [lane_spread(s_rows[i], 8 * k + j) for j in range(8)]
            t, v = s_rows[i], e_rows[i]
            for j in range(8):
                t = t - c[j] * ws[j]
                v = v - c[j] * we[j]
            s_rows[i], e_rows[i] = t, v
        for i in range(last, n):
            g = change[8 * (i - last) : 8 * (i - last) + 8]
            s_rows[i] = s_rows[i] - g[:, :128]
            e_rows[i] = e_rows[i] - g[:, 128:]
    return jnp.concatenate(upper, 0), jnp.concatenate(inverse, 0)


def unit(ref):
    row = lax.broadcasted_iota(jnp.int32, (NB, NB), 0)
    col = lax.broadcasted_iota(jnp.int32, (NB, NB), 1)
    ref[...] = jnp.where(row == col, 1.0, 0.0).astype(F32)


def factor_panel(p, s_ref, x_ref, u_ref, b_ref=None, lt_ref=None):
    base = pl.multiple_of(p * 128, 128)
    here = pl.ds(base, 128)
    rows = [s_ref[pl.ds(pl.multiple_of(base + 8 * i, 8), 8), here] for i in range(16)]
    upper, inverse = factor128(rows)
    across = dot(inverse, s_ref[here, :])
    place = lax.broadcasted_iota(jnp.int32, (128, NB), 1)
    u_ref[here, :] = jnp.where(place >= base + 128, across, 0.0)
    u_ref[here, here] = upper
    xrow = dot(inverse, x_ref[here, :])
    x_ref[here, :] = xrow
    if b_ref is not None:
        brow = dot(inverse, b_ref[here, :])
        lt_ref[here, :] = brow

    @pl.when(p < 3)
    def _():
        below = dot_nt(s_ref[:, here], inverse)
        place = lax.broadcasted_iota(jnp.int32, (NB, 128), 0)
        below = jnp.where(place >= base + 128, below, 0.0)
        s_ref[...] = s_ref[...] - dot(below, across)
        x_ref[...] = x_ref[...] - dot(below, xrow)
        if b_ref is not None:
            b_ref[...] = b_ref[...] - dot(below, brow)


def exchange_kernel(
    cov_ref, g_ref, r0_ref, c0_ref, x00_out, x11_out, u00_out, u11_out,
    s_ref, w_ref, u_ref, x11_ref, u11_ref, a10_ref, a11_ref, own_ref, blk_ref,
    local_sem, out_sem, pre_send, pre_recv, tz_send, tz_recv, sc_send, sc_recv, rs_send, tx_send, tx_recv, ts_send, ts_recv, sh_send, sh_recv, ta_send, ta_recv,
    row_send, row_recv, ag_send, ag_recv, sib_send, sib_recv, c_send, c_recv, near_send, near_recv,
):
    row = lax.axis_index("row")
    col = lax.axis_index("col")
    z, core = row // 2, row % 2
    y, x = col // 4, col % 4
    pos = {"x": x, "y": y, "z": z}

    def along(axis, delta):
        q = dict(pos)
        q[axis] = (q[axis] + delta) % 4
        return (q["z"] * 2 + core, q["y"] * 4 + q["x"])

    sibling = (z * 2 + (1 - core), col)

    def remote(src, dst, target, ssem, rsem):
        return pltpu.make_async_remote_copy(
            src_ref=src, dst_ref=dst, send_sem=ssem, recv_sem=rsem, device_id=target, device_id_type=MESH
        )

    def local(src, dst):
        c = pltpu.make_async_copy(src, dst, local_sem)
        c.start()
        c.wait()

    is_root = (row == 0) & (col == 0)
    source_col = (y % 2) * 8 + row
    w_ref[:, NB:] = jnp.zeros((NB, NB), F32)

    barrier = pltpu.get_barrier_semaphore()

    def greet(target):
        pl.semaphore_signal(barrier, inc=1, device_id=target, device_id_type=MESH)

    def spread_target(m, q):
        return (q * 2 + m, col)

    def spread_self(m, q):
        return q * 2 + m == row

    def row_target(m, q):
        l = 2 * m + col // 8
        return (col % 8, l * 4 + q), l

    def row_self(m, q):
        target, _ = row_target(m, q)
        return (target[0] == row) & (target[1] == col)

    for axis in "xyz":
        for delta in (1, 2, 3):
            greet(along(axis, delta))
    greet(sibling)
    for which in range(2):
        pl.when(row != which)(functools.partial(greet, (which, col)))
    pl.when(jnp.logical_not(is_root))(lambda: greet((0, source_col)))

    @pl.when(row < 2)
    def _():
        for m in range(2):
            for q in range(4):
                pl.when(jnp.logical_not(spread_self(m, q)))(functools.partial(greet, spread_target(m, q)))

    @pl.when(row == 0)
    def _():
        for m in range(2):
            for q in range(4):
                pl.when(jnp.logical_not(row_self(m, q)))(functools.partial(greet, row_target(m, q)[0]))

    first = (row == 0).astype(jnp.int32)
    second = (row == 1).astype(jnp.int32)
    root_i = is_root.astype(jnp.int32)
    pl.semaphore_wait(barrier, 10 + (2 - first - second) + (1 - root_i) + 7 * (first + second) + 8 * first - root_i)

    def quarter(m, q):
        return cov_ref.at[0, m, :, pl.ds(128 * q, 128)]

    def spread_copy(m, q, which):
        dst = c0_ref.at[m, q] if which == 0 else own_ref
        return remote(quarter(m, q), dst, spread_target(m, q), sc_send.at[m * 4 + q], sc_recv.at[which])

    def row_copy(m, q):
        target, l = row_target(m, q)
        return remote(quarter(m, q), r0_ref.at[l, q], target, rs_send.at[m * 4 + q], sc_recv.at[2])

    def tile_block(q):
        return a11_ref.at[:, pl.ds(pl.multiple_of(q * 128, 128), 128)]

    def hand_over(q):
        return remote(quarter(0, q), tile_block(q), (2 * q + 1, col), pre_send.at[q], pre_recv)

    def tile_to_root():
        return remote(cov_ref.at[0, 0], a10_ref, sibling, near_send.at[5], near_recv.at[5])

    @pl.when((row == 1) & (col == 0))
    def _():
        tile_to_root().start()

    @pl.when((row == 1) & (col == 1))
    def _():
        for q in range(1, 4):
            hand_over(q).start()

    for which in range(2):

        @pl.when(row == which)
        def _(which=which):
            for m in range(2):
                for q in range(4):
                    pl.when(jnp.logical_not(spread_self(m, q)))(spread_copy(m, q, which).start)

    @pl.when(row == 0)
    def _():
        local(quarter(0, 0), blk_ref)
        local(blk_ref, c0_ref.at[0, 0])

    @pl.when(row == 0)
    def _():
        for m in range(2):
            for q in range(4):
                pl.when(jnp.logical_not(row_self(m, q)))(row_copy(m, q).start)

    @pl.when(is_root)
    def _():
        local(blk_ref, r0_ref.at[0, 0])

    @pl.when(row == 1)
    def _():
        local(quarter(1, 0), own_ref)

    def level(order, root):
        found = -1
        for t, a in enumerate(order):
            found = jnp.where(pos[a] != root[a], t, found)
        return found

    def tree(parts, roots, piece, ssem, rsem):
        levels = [level(order, root) for (_, _, order), root in zip(parts, roots)]
        count = len(parts)
        depth = len(parts[0][2])

        def copy(i, t, k):
            r0, n, order = parts[i]
            return remote(piece(r0, n), piece(r0, n), along(order[t], k + 1), ssem(i, t * 3 + k), rsem(i))

        def begin(chosen=range(len(parts))):
            for t in range(depth):
                for i in chosen:
                    for k in range(3):
                        copy(i, t, k).start()

        def arrive(s):
            for i in range(count):

                @pl.when(levels[i] == s)
                def _(i=i):
                    copy(i, 0, 0).wait_recv()
                    for t in range(s + 1, depth):
                        for k in range(3):
                            copy(i, t, k).start()

        def sent():
            for i in range(count):
                for t in range(depth):

                    @pl.when(levels[i] < t)
                    def _(i=i, t=t):
                        for k in range(3):
                            copy(i, t, k).wait_send()

        return begin, arrive, sent, levels

    zero_root = {"x": 0, "y": 0, "z": 0}

    def panel_piece(p, r0, n):
        return w_ref.at[pl.ds(128 * p + r0, n), pl.ds(NB, 128 * (p + 1))]

    panel_trees = [
        tree(
            TREE_PANEL, [zero_root] * 3, functools.partial(panel_piece, p),
            lambda j, k, p=p: tx_send.at[p, j, k],
            lambda j, p=p: tx_recv.at[p, j],
        )
        for p in range(4)
    ]

    def panel_to_sibling(p):
        ref = panel_piece(p, 0, 128)
        return remote(ref, ref, sibling, near_send.at[p], near_recv.at[p])

    def side_piece(p, r0, n):
        return w_ref.at[pl.ds(128 * p + r0, n), pl.ds(0, NB)]

    side_trees = [
        tree(
            TREE_PANEL, [zero_root] * 3, functools.partial(side_piece, p),
            lambda j, k, p=p: ts_send.at[p, j, k],
            lambda j, p=p: ts_recv.at[p, j],
        )
        for p in range(4)
    ]

    def side_hand(p):
        return remote(
            a10_ref.at[pl.ds(128 * p, 128), :], side_piece(p, 0, 128), sibling, sh_send.at[p], sh_recv.at[p]
        )

    def side_to_sibling(p):
        ref = side_piece(p, 0, 128)
        return remote(ref, ref, sibling, near_send.at[6 + p], near_recv.at[6 + p])

    tile_begin, tile_arrive, tile_sent, _ = tree(
        TREE_BLOCK, [{"x": 1, "y": 0}] * 2,
        lambda r0, n: tile_block(z).at[pl.ds(r0, n), :],
        lambda j, k: ta_send.at[j, k],
        lambda j: ta_recv.at[j],
    )

    def tile_along(k):
        return remote(tile_block(z), tile_block(z), along("z", k + 1), tz_send.at[k], tz_recv.at[k])

    def tile_from(k):
        ref = tile_block((z + 3 - k) % 4)
        return remote(ref, ref, along("z", 3 - k), tz_send.at[k], tz_recv.at[k])

    def tile_to_sibling():
        return remote(a11_ref, a11_ref, sibling, near_send.at[4], near_recv.at[4])

    @pl.when(jnp.logical_not(is_root))
    def _():
        u_ref[...] = jnp.zeros((NB, NB), F32)

    @pl.when(is_root)
    def _():
        local(cov_ref.at[0, 0], s_ref)
        unit(x11_ref)
        tile_to_root().wait_recv()
        u11_ref[...] = a10_ref[...].T

    def gather(parts, view, own, ssem, rsem, sib=None):
        phases = len(parts[0][3])

        def part_view(order, k, delta, r0, n, c=core):
            at = {}
            for j, a in enumerate(order):
                if j < k:
                    at[a] = slice(None)
                elif j == k:
                    at[a] = (pos[a] + delta) % 4
                else:
                    at[a] = pos[a]
            return view(at, r0, n, c)

        def number(k, i):
            return (k * len(parts) + i) * 4

        def direct(k, i, j):
            r0, n, h, order = parts[i]
            m = number(k, i)
            dst = part_view(order, k, 0, r0, n)
            src = own(r0, n) if k == 0 else dst
            return remote(src, dst, along(order[k], (1, 3)[j]), ssem.at[m + j], rsem.at[m + j])

        def passed(k, i, j, back):
            r0, n, h, order = parts[i]
            m = number(k, i) + 2 + j
            q0, qn = ((r0, h), (r0 + h, n - h))[j]
            half = part_view(order, k, back, q0, qn)
            return remote(half, half, along(order[k], (1, 3)[j]), ssem.at[m], rsem.at[m])

        def send(k):
            for i in range(len(parts)):
                for j in range(2):
                    direct(k, i, j).start()

        def forward(k):
            for i, (r0, n, h, order) in enumerate(parts):
                m = number(k, i)
                for j, back in ((0, 3), (1, 1)):
                    got = part_view(order, k, back, r0, n)
                    remote(got, got, along(order[k], 1), ssem.at[m + j], rsem.at[m + j]).wait_recv()
                    passed(k, i, j, back).start()
                    if sib:
                        sib(got, 3 + k * 9 + i * 2 + j).start()

        def finish(k):
            for i, (r0, n, h, order) in enumerate(parts):
                for j in range(2):
                    passed(k, i, j, 2).wait_recv()
                if sib:
                    sib(part_view(order, k, 2, r0, n), 3 + k * 9 + 6 + i).start()

        def sent():
            for k in range(phases):
                for i in range(len(parts)):
                    for j in range(2):
                        direct(k, i, j).wait_send()
                        passed(k, i, j, 2).wait_send()

        def pair_views(c):
            views = [part_view(order, 0, 0, r0, n, c) for (r0, n, h, order) in parts]
            for k in range(phases):
                for r0, n, h, order in parts:
                    views.append(part_view(order, k, 3, r0, n, c))
                    views.append(part_view(order, k, 1, r0, n, c))
                for r0, n, h, order in parts:
                    views.append(part_view(order, k, 2, r0, n, c))
            return views

        return send, forward, finish, sent, pair_views

    row_send_step, row_forward, row_finish, row_sent, _ = gather(
        PARTS2,
        lambda at, r0, n, c: r0_ref.at[at["y"], at["x"], pl.ds(r0, n), :],
        lambda r0, n: r0_ref.at[y, x, pl.ds(r0, n), :],
        row_send, row_recv,
    )

    def row_begin():
        @pl.when(jnp.logical_not(is_root))
        def _():
            remote(r0_ref.at[y, x], r0_ref.at[y, x], (0, source_col), rs_send.at[0], sc_recv.at[2]).wait_recv()

        row_send_step(0)

    def chol_one(p, carry):
        factor_panel(p, s_ref, x11_ref, u_ref, u11_ref, a10_ref)
        here = pl.ds(pl.multiple_of(p * 128, 128), 128)
        w_ref[here, NB:] = x11_ref[here, :]
        for k in range(4):

            @pl.when(p == k)
            def _(k=k):
                side_hand(k).start()
                panel_trees[k][0]()
                panel_to_sibling(k).start()

        return carry

    @pl.when(is_root)
    def _():
        lax.fori_loop(0, 4, chol_one, 0)

    @pl.when((core == 0) & jnp.logical_not(is_root))
    def _():
        for p, s in SCHEDULE:
            panel_trees[p][1](s)
            if s == 2:
                panel_to_sibling(p).start()

    @pl.when(core == 0)
    def _():
        for p in range(4):
            side_to_sibling(p).wait_recv()

    @pl.when(core == 1)
    def _():
        @pl.when(col == 1)
        def _():
            pl.when(row == 1)(lambda: local(quarter(0, 0), tile_block(0)))
            pl.when(row != 1)(lambda: hand_over(z).wait_recv())
            tile_begin()

        is_hand = (row == 1) & (col == 0)

        @pl.when(is_hand)
        def _():
            for s in range(2):
                tile_arrive(s)
            for k in range(3):
                tile_along(k).start()
            for p in range(4):
                side_hand(p).wait_recv()
                side_trees[p][0]()
                side_to_sibling(p).start()

        @pl.when(jnp.logical_not(is_hand))
        def _():
            tile_arrive(0)
            for n, (p, s) in enumerate(SCHEDULE):
                side_trees[p][1](s)
                if s == 2:
                    side_to_sibling(p).start()
                if n == 0:
                    tile_arrive(1)
                    for k in range(3):
                        tile_along(k).start()

        for p in range(4):
            panel_to_sibling(p).wait_recv()

    for which in range(2):

        @pl.when(row != which)
        def _(which=which):
            ref = c0_ref.at[core, z] if which == 0 else own_ref
            remote(ref, ref, (which, col), sc_send.at[0], sc_recv.at[which]).wait_recv()

    local(c0_ref.at[core, z], blk_ref)
    lower10 = w_ref[:, :NB].T
    own_ref[...] = own_ref[...] - dot(lower10, dot(w_ref[:, NB:], blk_ref[...]))

    def to_sib(ref, i):
        return remote(ref, ref, sibling, sib_send.at[i], sib_recv.at[i])

    def own_part(r0, n):
        return own_ref.at[pl.ds(r0, n), :]

    send, forward, finish, sent, pair_views = gather(
        PARTS3,
        lambda at, r0, n, c: g_ref.at[at["z"], at["y"], at["x"], c, pl.ds(r0, n), :],
        own_part, ag_send, ag_recv, to_sib,
    )
    send(0)
    local(own_ref, g_ref.at[z, y, x, core])
    for i, (r0, n, h, order) in enumerate(PARTS3):
        to_sib(g_ref.at[z, y, x, core, pl.ds(r0, n), :], i).start()
    pltpu.make_async_copy(w_ref.at[:, pl.ds(NB, NB)], x00_out, out_sem.at[0]).start()
    def line_copy(k):
        ref = c0_ref.at[core, z]
        return remote(ref, ref, along("z", k + 1), c_send.at[k], c_recv.at[k])

    def line_from(k):
        ref = c0_ref.at[core, (z + 3 - k) % 4]
        return remote(ref, ref, along("z", 3 - k), c_send.at[k], c_recv.at[k])

    def line_to_sibling(m):
        return remote(c0_ref.at[m], c0_ref.at[m], sibling, c_send.at[3], c_recv.at[3])

    forward(0)
    finish(0)
    send(1)
    row_begin()
    for k in range(3):
        line_copy(k).start()
    forward(1)
    row_forward(0)
    finish(1)
    send(2)
    row_finish(0)
    row_send_step(1)

    @pl.when(core == 1)
    def _():
        for k in range(3):
            tile_from(k).wait_recv()
        tile_to_sibling().start()

    pl.when(core == 0)(lambda: tile_to_sibling().wait_recv())
    s_ref[...] = a11_ref[...] - dot(lower10, w_ref[:, :NB])
    unit(x11_ref)

    def chol_two(p, carry):
        factor_panel(p, s_ref, x11_ref, u11_ref)
        return carry

    lax.fori_loop(0, 4, chol_two, 0)
    pltpu.make_async_copy(x11_ref, x11_out, out_sem.at[1]).start()
    pltpu.make_async_copy(u11_ref, u11_out, out_sem.at[2]).start()
    pltpu.make_async_copy(u_ref, u00_out, out_sem.at[3]).start()
    row_forward(1)
    for k in range(3):
        line_from(k).wait_recv()
    line_to_sibling(core).start()
    forward(2)
    row_finish(1)
    finish(2)

    pltpu.make_async_copy(w_ref.at[:, pl.ds(NB, NB)], x00_out, out_sem.at[0]).wait()
    pltpu.make_async_copy(x11_ref, x11_out, out_sem.at[1]).wait()
    pltpu.make_async_copy(u11_ref, u11_out, out_sem.at[2]).wait()
    pltpu.make_async_copy(u_ref, u00_out, out_sem.at[3]).wait()
    sent()
    row_sent()
    for i, v in enumerate(pair_views(core)):
        to_sib(v, i).wait_send()
    for i, v in enumerate(pair_views(1 - core)):
        to_sib(v, i).wait_recv()

    @pl.when(core == 0)
    def _():
        for p in range(4):
            panel_trees[p][2]()
            panel_to_sibling(p).wait_send()

        @pl.when(is_root)
        def _():
            for p in range(4):
                side_hand(p).wait_send()

    @pl.when(core == 1)
    def _():
        for p in range(4):
            side_trees[p][2]()
            side_to_sibling(p).wait_send()
        tile_sent()
        for k in range(3):
            tile_along(k).wait_send()
        tile_to_sibling().wait_send()

        @pl.when((row == 1) & (col == 0))
        def _():
            tile_to_root().wait_send()

        @pl.when((row == 1) & (col == 1))
        def _():
            for q in range(1, 4):
                hand_over(q).wait_send()

    for k in range(3):
        line_copy(k).wait_send()
    line_to_sibling(core).wait_send()
    line_to_sibling(1 - core).wait_recv()

    @pl.when(row < 2)
    def _():
        for m in range(2):
            for q in range(4):
                pl.when(jnp.logical_not(spread_self(m, q)))(spread_copy(m, q, 1).wait_send)

    @pl.when(row == 0)
    def _():
        for m in range(2):
            for q in range(4):
                pl.when(jnp.logical_not(row_self(m, q)))(row_copy(m, q).wait_send)


def split(v):
    high = v.astype(BF16)
    return high, (v - high.astype(F32)).astype(BF16)


def dot16(a, b):
    return lax.dot_general(a, b, (((1,), (0,)), ((), ())), preferred_element_type=F32)


def left_parts(v):
    high, low = split(v)
    return jnp.concatenate([high, high, low], 1)


def right_parts(v):
    high, low = split(v)
    return jnp.concatenate([high, low, high], 0)


def finish_kernel(
    plan_ref, cov_ref, g_ref, r0_ref, c0_ref, x00_ref, x11_ref, u00_ref, u11_ref,
    f_ref, o_ref,
    x_buf, xt_ref, xb_ref, row_buf, col_buf, tile_buf, left_ref, right_ref, half_buf, out_buf, zero_buf,
    x_sem, row_sem, col_sem, tile_sem, f_sem, half_sem, o_sem,
):
    row = lax.axis_index("row")
    col = lax.axis_index("col")

    def panel_tile(i):
        return g_ref.at[:, (i % 16) // 4, i % 4, i // 16]

    def row_copy(l, k):
        src = r0_ref.at[l] if k == 0 else panel_tile(l * 8 + row)
        return pltpu.make_async_copy(src, row_buf.at[k, l], row_sem.at[k, l])

    def col_copy(m, k):
        src = c0_ref.at[m] if k == 0 else panel_tile(m * 16 + col)
        return pltpu.make_async_copy(src, col_buf.at[k, m], col_sem.at[k, m])

    def tile_copy(n):
        return pltpu.make_async_copy(cov_ref.at[n // 2, n % 2], tile_buf.at[n], tile_sem.at[n])

    def f_copy(n):
        return pltpu.make_async_copy(tile_buf.at[n], f_ref.at[n // 2, n % 2], f_sem.at[n])

    def place(n):
        return (n // 2) * 8 + row, (n % 2) * 16 + col

    def updated(n):
        i, j = place(n)
        return (j > 1) & (i >= j)

    def entry(s):
        t = plan_ref[s]
        u = jnp.maximum(t, 0)
        return t >= 0, u // 4, (u // 2) % 2, u % 2

    def half_copy(s):
        _, _, m, h = entry(s)
        src = g_ref.at[pl.ds(2 * h, 2), s // 4, s % 4, m]
        return pltpu.make_async_copy(src, half_buf.at[s % 2], half_sem.at[s % 2])

    def x_copy(k):
        return pltpu.make_async_copy((x00_ref, x11_ref)[k], x_buf.at[k], x_sem.at[k])

    for k in range(2):
        x_copy(k).start()
    for m in range(2):
        for k in range(2):
            col_copy(m, k).start()
    for l in range(4):
        for k in range(2):
            row_copy(l, k).start()
    for n in range(8):
        pl.when(updated(n))(tile_copy(n).start)
    pl.when(entry(0)[0])(lambda: half_copy(0).start())

    for k in range(2):
        x_copy(k).wait()
        xt_ref[k] = left_parts(x_buf[k, :HALF, :HALF])
        xb_ref[k] = left_parts(x_buf[k, HALF:, :])
    zero_buf[...] = jnp.zeros((NB, HALF), F32)

    def solved(k, blocks):
        tile = jnp.concatenate(blocks, 1)
        top = dot16(xt_ref[k], right_parts(tile[:HALF]))
        return jnp.concatenate([top, dot16(xb_ref[k], right_parts(tile))], 0)

    def make_col(m, carry):
        for k in range(2):
            col_copy(m, k).wait()
            right_ref[m, 3 * k * NB : 3 * (k + 1) * NB, :] = right_parts(
                solved(k, [col_buf[k, m, q] for q in range(4)])
            )
        return carry

    lax.fori_loop(0, 2, make_col, 0)

    def make_row(l, carry):
        for k in range(2):
            row_copy(l, k).wait()
            p = solved(k, [row_buf[k, l, q] for q in range(4)]).T
            left_ref[l, :, 3 * k * NB : 3 * (k + 1) * NB] = left_parts(p)
            i = l * 8 + row

            @pl.when(col == k)
            def _():
                tile_buf[2 * l] = p

                @pl.when(i == k)
                def _():
                    factor = pltpu.make_async_copy((u00_ref, u11_ref)[k], x_buf.at[k], x_sem.at[k])
                    factor.start()
                    factor.wait()
                    tile_buf[2 * l] = x_buf[k].T

                @pl.when(i < k)
                def _():
                    tile_buf[2 * l] = jnp.zeros((NB, NB), F32)

        return carry

    lax.fori_loop(0, 4, make_row, 0)

    def trailing(n, carry):
        i, j = place(n)
        l, m = n // 2, n % 2

        @pl.when(updated(n))
        def _():
            tile_copy(n).wait()
            tile_buf[n] = tile_buf[n] - dot16(left_ref[l], right_ref[m])

        @pl.when((j > 1) & (i < j))
        def _():
            tile_buf[n] = jnp.zeros((NB, NB), F32)

        f_copy(n).start()
        return carry

    lax.fori_loop(0, 8, trailing, 0)

    def out_copy(s):
        return pltpu.make_async_copy(out_buf.at[s % 2], o_ref.at[s], o_sem.at[s % 2])

    def moved(s, carry):
        live, l, m, h = entry(s)

        @pl.when(s >= 2)
        def _():
            out_copy(s).wait()

        @pl.when((s < 15) & entry(jnp.minimum(s + 1, 15))[0])
        def _():
            half_copy(jnp.minimum(s + 1, 15)).start()

        @pl.when(live)
        def _():
            half_copy(s).wait()
            right = right_parts(solved(1, [half_buf[s % 2, q] for q in range(2)]))
            out_buf[s % 2] = dot16(left_ref[l, :, 3 * NB :], right)
            out_copy(s).start()

        @pl.when(jnp.logical_not(live))
        def _():
            pltpu.make_async_copy(zero_buf, o_ref.at[s], o_sem.at[s % 2]).start()

        return carry

    lax.fori_loop(0, 16, moved, 0)
    for s in (14, 15):
        out_copy(s).wait()
    for n in range(8):
        f_copy(n).wait()


def per_device(covariance, migration):
    cov = covariance.reshape(4, 2, NB, NB)
    row = lax.axis_index("row")
    col = lax.axis_index("col")
    plan = lax.dynamic_slice(migration, (row, 0, col), (1, 16, 1)).reshape(16)
    dma = pltpu.SemaphoreType.DMA
    square = jax.ShapeDtypeStruct((NB, NB), F32)
    g, r0, c0, x00, x11, u00, u11 = pl.pallas_call(
        exchange_kernel,
        out_shape=[
            jax.ShapeDtypeStruct((4, 4, 4, 2, NB, QB), F32),
            jax.ShapeDtypeStruct((4, 4, NB, QB), F32),
            jax.ShapeDtypeStruct((2, 4, NB, QB), F32),
            square, square, square, square,
        ],
        in_specs=[ANY],
        out_specs=[ANY] * 7,
        scratch_shapes=[pltpu.VMEM((NB, NB), F32), pltpu.VMEM((NB, 2 * NB), F32)]
        + [pltpu.VMEM((NB, NB), F32)] * 5
        + [pltpu.VMEM((NB, QB), F32)] * 2
        + [
            dma, dma((4,)), dma((4,)), dma, dma((3,)), dma((3,)), dma((8,)), dma((3,)), dma((8,)),
            dma((4, 3, 9)), dma((4, 3)), dma((4, 3, 9)), dma((4, 3)), dma((4,)), dma((4,)), dma((2, 6)), dma((2,)),
            dma((16,)), dma((16,)), dma((36,)), dma((36,)), dma((30,)), dma((30,)),
            dma((4,)), dma((4,)), dma((10,)), dma((10,)),
        ],
        compiler_params=pltpu.CompilerParams(
            collective_id=0, has_side_effects=True, vmem_limit_bytes=48 * 2**20
        ),
        name="exchange",
    )(cov)
    factor, offloaded = pl.pallas_call(
        finish_kernel,
        out_shape=[
            jax.ShapeDtypeStruct((4, 2, NB, NB), F32),
            jax.ShapeDtypeStruct((16, NB, HALF), F32),
        ],
        in_specs=[SMEM] + [ANY] * 8,
        out_specs=[ANY, ANY],
        scratch_shapes=[
            pltpu.VMEM((2, NB, NB), F32), pltpu.VMEM((2, HALF, 3 * HALF), BF16), pltpu.VMEM((2, HALF, 3 * NB), BF16),
            pltpu.VMEM((2, 4, 4, NB, QB), F32), pltpu.VMEM((2, 2, 4, NB, QB), F32),
            pltpu.VMEM((8, NB, NB), F32),
            pltpu.VMEM((4, NB, 6 * NB), BF16), pltpu.VMEM((2, 6 * NB, NB), BF16),
            pltpu.VMEM((2, 2, NB, QB), F32), pltpu.VMEM((2, NB, HALF), F32), pltpu.VMEM((NB, HALF), F32),
            dma((2,)), dma((2, 4)), dma((2, 2)), dma((8,)), dma((8,)), dma((2,)), dma((2,)),
        ],
        compiler_params=pltpu.CompilerParams(vmem_limit_bytes=60 * 2**20),
        name="finish",
    )(plan, cov, g, r0, c0, x00, x11, u00, u11)
    return factor[:, None, :, None], offloaded[None, None]


def solution(mesh):
    return jax.shard_map(
        per_device,
        mesh=mesh,
        in_specs=(P(None, "row", None, "col", None, None), P()),
        out_specs=(P(None, "row", None, "col", None, None), P("row", "col", None, None, None)),
        check_vma=False,
    )
```

time: 310 us -> 244 us (0.79)
  the two profiles are of different devices: /device:TPU:41 before, /device:TPU:103 now
where the time goes in v2:
time: 244 us
  Pallas kernels  237 us (97%)
  local copies, waits for them, and re-layouts  5.56 us (2%)
    pallas_call x1, Pallas kernels, per_device(): pl.pallas_call(exchange_kernel, out_shape=[jax.ShapeDtypeStruct((4, 4, 4,...  191 us
    pallas_call x1, Pallas kernels, per_device(): pl.pallas_call(finish_kernel, out_shape=[jax.ShapeDtypeStruct((4, 2, NB,...  46.2 us

profile of v2, /device:TPU:103, one launch (start us, length us, event | category | flops | bytes accessed | tf_op | source)
XLA Modules:
  0.0 243.6 jit_solution(1703956839832003417)
XLA Ops:
  0.6 0.0 copy-start
  0.7 0.8 copy-done
  1.5 0.8 dynamic-slice_reduce_fusion.plan_ref
  2.2 191.0 %exchange.1 = (f32[4,4,4,2,512,128]{5,4,3,2,1,0:T(8,128)}, f32[4,4,512,128]{3,2,1,0:T(8,128)}, f32[2,4,512,128]{3,2,1,0:T(8,128)}, f32[512,512]{1,0:T(8,128)S(1)...) custom-call(f32[4,2,512,512]{3,2,1,0:T(8,128)} %bitcast.5), custom_call_target="tpu_custom_call" | custom-call | tf_op jit(solution)/shard_map/exchange/pallas_call | solution.py:865
  193.2 0.0 copy-start.2
  193.2 1.0 copy-done.2
  194.2 0.0 copy-start.3
  194.2 1.0 copy-done.3
  195.2 0.0 copy-start.4
  195.2 1.0 copy-done.4
  196.2 0.0 copy-start.5
  196.2 1.0 copy-done.5
  197.2 0.0 copy-start.1
  197.2 46.2 %finish.1 = (f32[4,2,512,512]{3,2,1,0:T(8,128)}, f32[16,512,256]{2,1,0:T(8,128)}) custom-call(s32[16]{0:T(128)} %dynamic-slice_reduce_fusion.plan_ref, f32[4,2,512,512]{3,2,1,0:T(8,128)} %bitcast.6, f32[4,4,4,2,512,128]{5,4,3,2,1,0:T(8,128)} %get-tuple-element.11.g_ref, f32[4,4,512,128]{3,2,1,0:T(8,128)} %get-tuple-element.12.r0_ref, ...), custom_call_target="tpu_custom_call" | custom-call | tf_op jit(solution)/shard_map/finish/pallas_call | solution.py:889
  243.4 0.0 copy-done.1
Async XLA Ops:
  0.6 0.8 copy-start
  193.2 1.0 copy-start.2
  194.2 1.0 copy-start.3
  195.2 1.0 copy-start.4
  196.2 1.0 copy-start.5
  197.2 46.2 %copy-start.1 = (s32[8,16,16]{2,1,0:T(8,128)S(1)}, s32[8,16,16]{2,1,0:T(8,128)}, u32[]{:S(2)}) copy-start(s32[8,16,16]{2,1,0:T(8,128)} %param.3) | copy-start | bytes 24580

commit v3 on v2

--- a/solution.py
+++ b/solution.py
@@ -23,7 +23,6 @@
 TREE_BLOCK = ((0, 256, "xy"), (256, 256, "yx"))
 TREE_PANEL = ((0, 48, "xyz"), (48, 40, "yzx"), (88, 40, "zxy"))
 AHEAD = 2
-SCHEDULE = sorted(((p, s) for p in range(4) for s in range(3)), key=lambda v: 5.5 * v[0] + 6.0 * v[1])
 
 
 def dot(a, b):
@@ -123,7 +122,7 @@
     ref[...] = jnp.where(row == col, 1.0, 0.0).astype(F32)
 
 
-def factor_panel(p, s_ref, x_ref, u_ref, b_ref=None, lt_ref=None):
+def factor_panel(p, s_ref, x_ref, u_ref):
     base = pl.multiple_of(p * 128, 128)
     here = pl.ds(base, 128)
     rows = [s_ref[pl.ds(pl.multiple_of(base + 8 * i, 8), 8), here] for i in range(16)]
@@ -134,9 +133,6 @@
     u_ref[here, here] = upper
     xrow = dot(inverse, x_ref[here, :])
     x_ref[here, :] = xrow
-    if b_ref is not None:
-        brow = dot(inverse, b_ref[here, :])
-        lt_ref[here, :] = brow
 
     @pl.when(p < 3)
     def _():
@@ -145,14 +141,12 @@
         below = jnp.where(place >= base + 128, below, 0.0)
         s_ref[...] = s_ref[...] - dot(below, across)
         x_ref[...] = x_ref[...] - dot(below, xrow)
-        if b_ref is not None:
-            b_ref[...] = b_ref[...] - dot(below, brow)
 
 
 def exchange_kernel(
     cov_ref, g_ref, r0_ref, c0_ref, x00_out, x11_out, u00_out, u11_out,
-    s_ref, w_ref, u_ref, x11_ref, u11_ref, a10_ref, a11_ref, own_ref, blk_ref,
-    local_sem, out_sem, pre_send, pre_recv, tz_send, tz_recv, sc_send, sc_recv, rs_send, tx_send, tx_recv, ts_send, ts_recv, sh_send, sh_recv, ta_send, ta_recv,
+    s_ref, x_ref, u_ref, x11_ref, u11_ref, a10_ref, a11_ref, own_ref, blk_ref,
+    local_sem, pre_send, pre_recv, tz_send, tz_recv, sc_send, sc_recv, rs_send, tx_send, tx_recv, ta_send, ta_recv,
     row_send, row_recv, ag_send, ag_recv, sib_send, sib_recv, c_send, c_recv, near_send, near_recv,
 ):
     row = lax.axis_index("row")
@@ -180,7 +174,7 @@
 
     is_root = (row == 0) & (col == 0)
     source_col = (y % 2) * 8 + row
-    w_ref[:, NB:] = jnp.zeros((NB, NB), F32)
+    x_ref[...] = jnp.zeros((NB, NB), F32)
 
     barrier = pltpu.get_barrier_semaphore()
 
@@ -237,23 +231,18 @@
         target, l = row_target(m, q)
         return remote(quarter(m, q), r0_ref.at[l, q], target, rs_send.at[m * 4 + q], sc_recv.at[2])
 
-    def tile_block(q):
-        return a11_ref.at[:, pl.ds(pl.multiple_of(q * 128, 128), 128)]
-
-    def hand_over(q):
-        return remote(quarter(0, q), tile_block(q), (2 * q + 1, col), pre_send.at[q], pre_recv)
-
-    def tile_to_root():
-        return remote(cov_ref.at[0, 0], a10_ref, sibling, near_send.at[5], near_recv.at[5])
-
-    @pl.when((row == 1) & (col == 0))
-    def _():
-        tile_to_root().start()
-
-    @pl.when((row == 1) & (col == 1))
-    def _():
-        for q in range(1, 4):
-            hand_over(q).start()
+    def tile_block(i, q):
+        return (a10_ref, a11_ref)[i].at[:, pl.ds(pl.multiple_of(q * 128, 128), 128)]
+
+    def hand_over(i, q):
+        return remote(quarter(0, q), tile_block(i, q), (2 * q + 1, col), pre_send.at[q], pre_recv.at[i])
+
+    for i in range(2):
+
+        @pl.when((row == 1) & (col == i))
+        def _(i=i):
+            for q in range(1, 4):
+                hand_over(i, q).start()
 
     for which in range(2):
 
@@ -265,14 +254,11 @@
 
     @pl.when(row == 0)
     def _():
-        local(quarter(0, 0), blk_ref)
-        local(blk_ref, c0_ref.at[0, 0])
-
-    @pl.when(row == 0)
-    def _():
         for m in range(2):
             for q in range(4):
                 pl.when(jnp.logical_not(row_self(m, q)))(row_copy(m, q).start)
+        local(quarter(0, 0), blk_ref)
+        local(blk_ref, c0_ref.at[0, 0])
 
     @pl.when(is_root)
     def _():
@@ -297,9 +283,9 @@
             r0, n, order = parts[i]
             return remote(piece(r0, n), piece(r0, n), along(order[t], k + 1), ssem(i, t * 3 + k), rsem(i))
 
-        def begin(chosen=range(len(parts))):
+        def begin():
             for t in range(depth):
-                for i in chosen:
+                for i in range(count):
                     for k in range(3):
                         copy(i, t, k).start()
 
@@ -327,7 +313,7 @@
     zero_root = {"x": 0, "y": 0, "z": 0}
 
     def panel_piece(p, r0, n):
-        return w_ref.at[pl.ds(128 * p + r0, n), pl.ds(NB, 128 * (p + 1))]
+        return x_ref.at[pl.ds(128 * p + r0, n), pl.ds(0, 128 * (p + 1))]
 
     panel_trees = [
         tree(
@@ -342,54 +328,31 @@
         ref = panel_piece(p, 0, 128)
         return remote(ref, ref, sibling, near_send.at[p], near_recv.at[p])
 
-    def side_piece(p, r0, n):
-        return w_ref.at[pl.ds(128 * p + r0, n), pl.ds(0, NB)]
-
-    side_trees = [
+    tile_trees = [
         tree(
-            TREE_PANEL, [zero_root] * 3, functools.partial(side_piece, p),
-            lambda j, k, p=p: ts_send.at[p, j, k],
-            lambda j, p=p: ts_recv.at[p, j],
+            TREE_BLOCK, [{"x": i, "y": 0}] * 2,
+            lambda r0, n, i=i: tile_block(i, z).at[pl.ds(r0, n), :],
+            lambda j, k, i=i: ta_send.at[i, j, k],
+            lambda j, i=i: ta_recv.at[i, j],
         )
-        for p in range(4)
+        for i in range(2)
     ]
 
-    def side_hand(p):
-        return remote(
-            a10_ref.at[pl.ds(128 * p, 128), :], side_piece(p, 0, 128), sibling, sh_send.at[p], sh_recv.at[p]
-        )
-
-    def side_to_sibling(p):
-        ref = side_piece(p, 0, 128)
-        return remote(ref, ref, sibling, near_send.at[6 + p], near_recv.at[6 + p])
-
-    tile_begin, tile_arrive, tile_sent, _ = tree(
-        TREE_BLOCK, [{"x": 1, "y": 0}] * 2,
-        lambda r0, n: tile_block(z).at[pl.ds(r0, n), :],
-        lambda j, k: ta_send.at[j, k],
-        lambda j: ta_recv.at[j],
-    )
-
-    def tile_along(k):
-        return remote(tile_block(z), tile_block(z), along("z", k + 1), tz_send.at[k], tz_recv.at[k])
-
-    def tile_from(k):
-        ref = tile_block((z + 3 - k) % 4)
-        return remote(ref, ref, along("z", 3 - k), tz_send.at[k], tz_recv.at[k])
-
-    def tile_to_sibling():
-        return remote(a11_ref, a11_ref, sibling, near_send.at[4], near_recv.at[4])
-
-    @pl.when(jnp.logical_not(is_root))
-    def _():
-        u_ref[...] = jnp.zeros((NB, NB), F32)
+    def tile_along(i, k):
+        return remote(tile_block(i, z), tile_block(i, z), along("z", k + 1), tz_send.at[i, k], tz_recv.at[i, k])
+
+    def tile_from(i, k):
+        ref = tile_block(i, (z + 3 - k) % 4)
+        return remote(ref, ref, along("z", 3 - k), tz_send.at[i, k], tz_recv.at[i, k])
+
+    def tile_to_sibling(i):
+        ref = (a10_ref, a11_ref)[i]
+        return remote(ref, ref, sibling, near_send.at[4 + i], near_recv.at[4 + i])
 
     @pl.when(is_root)
     def _():
         local(cov_ref.at[0, 0], s_ref)
         unit(x11_ref)
-        tile_to_root().wait_recv()
-        u11_ref[...] = a10_ref[...].T
 
     def gather(parts, view, own, ssem, rsem, sib=None):
         phases = len(parts[0][3])
@@ -478,14 +441,13 @@
         row_send_step(0)
 
     def chol_one(p, carry):
-        factor_panel(p, s_ref, x11_ref, u_ref, u11_ref, a10_ref)
+        factor_panel(p, s_ref, x11_ref, u_ref)
         here = pl.ds(pl.multiple_of(p * 128, 128), 128)
-        w_ref[here, NB:] = x11_ref[here, :]
+        x_ref[here, :] = x11_ref[here, :]
         for k in range(4):
 
             @pl.when(p == k)
             def _(k=k):
-                side_hand(k).start()
                 panel_trees[k][0]()
                 panel_to_sibling(k).start()
 
@@ -497,51 +459,46 @@
 
     @pl.when((core == 0) & jnp.logical_not(is_root))
     def _():
-        for p, s in SCHEDULE:
+        for p, s in (
+            (0, 0), (0, 1), (1, 0), (0, 2), (1, 1), (2, 0), (1, 2), (2, 1), (3, 0), (2, 2), (3, 1), (3, 2)
+        ):
             panel_trees[p][1](s)
             if s == 2:
                 panel_to_sibling(p).start()
 
-    @pl.when(core == 0)
-    def _():
-        for p in range(4):
-            side_to_sibling(p).wait_recv()
-
     @pl.when(core == 1)
     def _():
-        @pl.when(col == 1)
-        def _():
-            pl.when(row == 1)(lambda: local(quarter(0, 0), tile_block(0)))
-            pl.when(row != 1)(lambda: hand_over(z).wait_recv())
-            tile_begin()
-
-        is_hand = (row == 1) & (col == 0)
-
-        @pl.when(is_hand)
-        def _():
-            for s in range(2):
-                tile_arrive(s)
+        for i in range(2):
+
+            @pl.when(col == i)
+            def _(i=i):
+                @pl.when(row == 1)
+                def _():
+                    local(quarter(0, 0), tile_block(i, 0))
+
+                @pl.when(row != 1)
+                def _():
+                    hand_over(i, z).wait_recv()
+
+                tile_trees[i][0]()
+
+        for s in range(2):
+            for i in range(2):
+                tile_trees[i][1](s)
+        for i in range(2):
             for k in range(3):
-                tile_along(k).start()
-            for p in range(4):
-                side_hand(p).wait_recv()
-                side_trees[p][0]()
-                side_to_sibling(p).start()
-
-        @pl.when(jnp.logical_not(is_hand))
-        def _():
-            tile_arrive(0)
-            for n, (p, s) in enumerate(SCHEDULE):
-                side_trees[p][1](s)
-                if s == 2:
-                    side_to_sibling(p).start()
-                if n == 0:
-                    tile_arrive(1)
-                    for k in range(3):
-                        tile_along(k).start()
-
+                tile_along(i, k).start()
+        for i in range(2):
+            for k in range(3):
+                tile_from(i, k).wait_recv()
+            tile_to_sibling(i).start()
         for p in range(4):
             panel_to_sibling(p).wait_recv()
+
+    @pl.when(core == 0)
+    def _():
+        for i in range(2):
+            tile_to_sibling(i).wait_recv()
 
     for which in range(2):
 
@@ -551,8 +508,9 @@
             remote(ref, ref, (which, col), sc_send.at[0], sc_recv.at[which]).wait_recv()
 
     local(c0_ref.at[core, z], blk_ref)
-    lower10 = w_ref[:, :NB].T
-    own_ref[...] = own_ref[...] - dot(lower10, dot(w_ref[:, NB:], blk_ref[...]))
+    lower10 = dot_nt(a10_ref[...], x_ref[...])
+    own_ref[...] = own_ref[...] - dot(lower10, dot(x_ref[...], blk_ref[...]))
+    s11 = a11_ref[...] - dot_nt(lower10, lower10)
 
     def to_sib(ref, i):
         return remote(ref, ref, sibling, sib_send.at[i], sib_recv.at[i])
@@ -569,7 +527,10 @@
     local(own_ref, g_ref.at[z, y, x, core])
     for i, (r0, n, h, order) in enumerate(PARTS3):
         to_sib(g_ref.at[z, y, x, core, pl.ds(r0, n), :], i).start()
-    pltpu.make_async_copy(w_ref.at[:, pl.ds(NB, NB)], x00_out, out_sem.at[0]).start()
+    s_ref[...] = s11
+    unit(x11_ref)
+    row_begin()
+
     def line_copy(k):
         ref = c0_ref.at[core, z]
         return remote(ref, ref, along("z", k + 1), c_send.at[k], c_recv.at[k])
@@ -584,46 +545,40 @@
     forward(0)
     finish(0)
     send(1)
-    row_begin()
     for k in range(3):
         line_copy(k).start()
-    forward(1)
     row_forward(0)
-    finish(1)
-    send(2)
     row_finish(0)
     row_send_step(1)
 
-    @pl.when(core == 1)
-    def _():
-        for k in range(3):
-            tile_from(k).wait_recv()
-        tile_to_sibling().start()
-
-    pl.when(core == 0)(lambda: tile_to_sibling().wait_recv())
-    s_ref[...] = a11_ref[...] - dot(lower10, w_ref[:, :NB])
-    unit(x11_ref)
-
     def chol_two(p, carry):
         factor_panel(p, s_ref, x11_ref, u11_ref)
+
+        @pl.when(p == 1)
+        def _():
+            forward(1)
+
+        @pl.when(p == 2)
+        def _():
+            finish(1)
+            send(2)
+            row_forward(1)
+
         return carry
 
     lax.fori_loop(0, 4, chol_two, 0)
-    pltpu.make_async_copy(x11_ref, x11_out, out_sem.at[1]).start()
-    pltpu.make_async_copy(u11_ref, u11_out, out_sem.at[2]).start()
-    pltpu.make_async_copy(u_ref, u00_out, out_sem.at[3]).start()
-    row_forward(1)
+    row_finish(1)
     for k in range(3):
         line_from(k).wait_recv()
     line_to_sibling(core).start()
     forward(2)
-    row_finish(1)
     finish(2)
 
-    pltpu.make_async_copy(w_ref.at[:, pl.ds(NB, NB)], x00_out, out_sem.at[0]).wait()
-    pltpu.make_async_copy(x11_ref, x11_out, out_sem.at[1]).wait()
-    pltpu.make_async_copy(u11_ref, u11_out, out_sem.at[2]).wait()
-    pltpu.make_async_copy(u_ref, u00_out, out_sem.at[3]).wait()
+    x00_out[...] = x_ref[...]
+    x11_out[...] = x11_ref[...]
+    u00_out[...] = u_ref[...]
+    u11_out[...] = u11_ref[...]
+
     sent()
     row_sent()
     for i, v in enumerate(pair_views(core)):
@@ -637,29 +592,18 @@
             panel_trees[p][2]()
             panel_to_sibling(p).wait_send()
 
-        @pl.when(is_root)
-        def _():
-            for p in range(4):
-                side_hand(p).wait_send()
-
     @pl.when(core == 1)
     def _():
-        for p in range(4):
-            side_trees[p][2]()
-            side_to_sibling(p).wait_send()
-        tile_sent()
-        for k in range(3):
-            tile_along(k).wait_send()
-        tile_to_sibling().wait_send()
-
-        @pl.when((row == 1) & (col == 0))
-        def _():
-            tile_to_root().wait_send()
-
-        @pl.when((row == 1) & (col == 1))
-        def _():
-            for q in range(1, 4):
-                hand_over(q).wait_send()
+        for i in range(2):
+            tile_trees[i][2]()
+            for k in range(3):
+                tile_along(i, k).wait_send()
+            tile_to_sibling(i).wait_send()
+
+            @pl.when((row == 1) & (col == i))
+            def _(i=i):
+                for q in range(1, 4):
+                    hand_over(i, q).wait_send()
 
     for k in range(3):
         line_copy(k).wait_send()
@@ -871,15 +815,14 @@
             square, square, square, square,
         ],
         in_specs=[ANY],
-        out_specs=[ANY] * 7,
-        scratch_shapes=[pltpu.VMEM((NB, NB), F32), pltpu.VMEM((NB, 2 * NB), F32)]
-        + [pltpu.VMEM((NB, NB), F32)] * 5
+        out_specs=[ANY] * 3 + [VMEM] * 4,
+        scratch_shapes=[pltpu.VMEM((NB, NB), F32)] * 7
         + [pltpu.VMEM((NB, QB), F32)] * 2
         + [
-            dma, dma((4,)), dma((4,)), dma, dma((3,)), dma((3,)), dma((8,)), dma((3,)), dma((8,)),
-            dma((4, 3, 9)), dma((4, 3)), dma((4, 3, 9)), dma((4, 3)), dma((4,)), dma((4,)), dma((2, 6)), dma((2,)),
+            dma, dma((4,)), dma((2,)), dma((2, 3)), dma((2, 3)), dma((8,)), dma((3,)), dma((8,)),
+            dma((4, 3, 9)), dma((4, 3)), dma((2, 2, 6)), dma((2, 2)),
             dma((16,)), dma((16,)), dma((36,)), dma((36,)), dma((30,)), dma((30,)),
-            dma((4,)), dma((4,)), dma((10,)), dma((10,)),
+            dma((4,)), dma((4,)), dma((6,)), dma((6,)),
         ],
         compiler_params=pltpu.CompilerParams(
             collective_id=0, has_side_effects=True, vmem_limit_bytes=48 * 2**20

time: 244 us -> 236 us (0.967)
  Pallas kernels: 237 us -> 228 us
    pallas_call x1, Pallas kernels: 191 us -> 183 us  [per_device(): pl.pallas_call(exchange_kernel, out_shape=[jax.ShapeDtypeStruct((4, 4, 4,...]
where the time goes in v3:
time: 236 us; the launch traced here: 235 us
  Pallas kernels  228 us (97%)
  local copies, waits for them, and re-layouts  5.56 us (2%)
    pallas_call x1, Pallas kernels, per_device(): pl.pallas_call(exchange_kernel, out_shape=[jax.ShapeDtypeStruct((4, 4, 4,...  183 us
    pallas_call x1, Pallas kernels, per_device(): pl.pallas_call(finish_kernel, out_shape=[jax.ShapeDtypeStruct((4, 2, NB,...  45 us
    unnamed x12, local copies, waits for them, and re-layouts  4.79 us

profile of v3, /device:TPU:103, one launch (start us, length us, event | category | flops | bytes accessed | tf_op | source)
XLA Modules:
  0.0 234.7 jit_solution(2891485084656986117)
XLA Ops:
  0.6 0.0 copy-start
  0.7 0.8 copy-done
  1.5 0.8 dynamic-slice_reduce_fusion.plan_ref
  2.2 183.3 %exchange.1 = (f32[4,4,4,2,512,128]{5,4,3,2,1,0:T(8,128)}, f32[4,4,512,128]{3,2,1,0:T(8,128)}, f32[2,4,512,128]{3,2,1,0:T(8,128)}, f32[512,512]{1,0:T(8,128)S(1)...) custom-call(f32[4,2,512,512]{3,2,1,0:T(8,128)} %bitcast.5), custom_call_target="tpu_custom_call" | custom-call | tf_op jit(solution)/shard_map/exchange/pallas_call | solution.py:809
  185.5 0.0 copy-start.2
  185.5 1.0 copy-done.2
  186.5 0.0 copy-start.3
  186.5 1.0 copy-done.3
  187.5 0.0 copy-start.4
  187.5 1.0 copy-done.4
  188.5 0.0 copy-start.5
  188.5 1.0 copy-done.5
  189.5 0.0 copy-start.1
  189.5 45.0 %finish.1 = (f32[4,2,512,512]{3,2,1,0:T(8,128)}, f32[16,512,256]{2,1,0:T(8,128)}) custom-call(s32[16]{0:T(128)} %dynamic-slice_reduce_fusion.plan_ref, f32[4,2,512,512]{3,2,1,0:T(8,128)} %bitcast.6, f32[4,4,4,2,512,128]{5,4,3,2,1,0:T(8,128)} %get-tuple-element.11.g_ref, f32[4,4,512,128]{3,2,1,0:T(8,128)} %get-tuple-element.12.r0_ref, ...), custom_call_target="tpu_custom_call" | custom-call | tf_op jit(solution)/shard_map/finish/pallas_call | solution.py:832
  234.5 0.0 copy-done.1
Async XLA Ops:
  0.6 0.8 copy-start
  185.5 1.0 copy-start.2
  186.5 1.0 copy-start.3
  187.5 1.0 copy-start.4
  188.5 1.0 copy-start.5
  189.5 45.0 %copy-start.1 = (s32[8,16,16]{2,1,0:T(8,128)S(1)}, s32[8,16,16]{2,1,0:T(8,128)}, u32[]{:S(2)}) copy-start(s32[8,16,16]{2,1,0:T(8,128)} %param.3) | copy-start | bytes 24580
